TPU v7x, 128 devices: a whole 4x4x4 slice. The times are simulated.
128 devices in a mesh: src: 4 (over x_lo, core), tgt: 32 (over z, y, x_hi).
Axes of the slice: x: 4 (x_hi: 2, x_lo: 2; x = x_hi * 2 + x_lo), y: 4, z: 4, core: 2. Of those that a mesh axis runs over, the one named last changes fastest.
Arguments:
- src_features: float32 [50, 32768], P(None, 'src'), may hold values from -6 to 6
- src_mass: float32 [32768], P('src'), may hold values from 6.1035157e-06 to 0.00061035156
- section_ids: int32 [32768], P('src'), may hold values from 0 to 31
- shard_counts: int32 [4], replicated, may hold values from 1 to 8192, 16384 in all
- section_offsets: float32 [50, 32], replicated, may hold values from -0.3125 to 0.3125
- tgt_features: float32 [50, 32768], P(None, 'tgt'), may hold values from -6 to 6
- tgt_mass: float32 [32768], P('tgt'), may hold values from 3.0517579e-06 to 0.00030517578
Outputs:
- src_potential: float32 [16384], P('src')
- tgt_potential: float32 [32768], P('tgt')
- self_potential: float32 [16384], P('src')
Inputs may be any that keep to these rules, and one draw needn't show every extreme that they name: The entries sum to 16384 and the largest equals 8192; block k uses its first shard_counts[k] slots.
All inputs are finite; a program needn't handle non-finite values.
Results may differ from a plain program's by a relative error of at most 0.0003.
Values sent between devices are 32-bit elements; how exact they have to be, the bound alone decides.
A program may use at most 64 MiB of HBM per device.

v0:
```python
import jax
import jax.numpy as jnp
from jax import lax
from jax.sharding import PartitionSpec as P

SECTIONS = 32
ITERS = 3
S_DEV = 4096
CAP = 8192


EPS = 0.05
TAU = 1.0 / (1.0 + EPS)
HIGH = lax.Precision.HIGHEST


def from_root(value, axis, source):
    kept = jnp.where(lax.axis_index(axis) == source, value, 0).astype(value.dtype)
    return lax.psum(kept, axis)


def tile_cost(xa, sqa, xb, sqb):
    cross = lax.dot_general(
        xa, xb, (((0,), (0,)), ((), ())), precision=HIGH, preferred_element_type=jnp.float32
    )
    return sqa[:, None] + sqb[None, :] - 2.0 * cross


def split_blocks(xa, sqa, weight):
    rows = xa.shape[1]
    size = min(512, rows)
    count = rows // size
    blocks = xa.reshape(xa.shape[0], count, size).transpose(1, 0, 2)
    return (blocks, sqa.reshape(count, size), weight.reshape(count, size))


def row_partials(xa, sqa, xb, sqb, weight):
    blocks, sq_blocks, unused = split_blocks(xa, sqa, sqa)

    def one(item):
        scores = weight[None, :] - tile_cost(item[0], item[1], xb, sqb) / EPS
        peak = jnp.max(scores, axis=1)
        return (peak, jnp.sum(jnp.exp(scores - peak[:, None]), axis=1))

    peak, total = lax.map(one, (blocks, sq_blocks))
    return (peak.reshape(-1), total.reshape(-1))


def column_partials(xa, sqa, xb, sqb, weight):
    blocks, sq_blocks, w_blocks = split_blocks(xa, sqa, weight)

    def step(carry, item):
        scores = item[2][:, None] - tile_cost(item[0], item[1], xb, sqb) / EPS
        peak = jnp.maximum(carry[0], jnp.max(scores, axis=0))
        total = carry[1] * jnp.exp(carry[0] - peak) + jnp.sum(
            jnp.exp(scores - peak[None, :]), axis=0
        )
        return ((peak, total), None)

    start = (jnp.full((xb.shape[1],), -1e30, jnp.float32), jnp.zeros((xb.shape[1],), jnp.float32))
    result, unused = lax.scan(step, start, (blocks, sq_blocks, w_blocks))
    return result


def reduce_rows(f_peak, f_total, p_peak, p_total):
    peaks = lax.pmax((f_peak, p_peak), "tgt")
    totals = lax.psum(
        (f_total * jnp.exp(f_peak - peaks[0]), p_total * jnp.exp(p_peak - peaks[1])), "tgt"
    )
    return (peaks[0] + jnp.log(totals[0]), peaks[1] + jnp.log(totals[1]))


def reduce_columns(peak, total):
    largest = lax.pmax(peak, "src")
    summed = lax.psum(total * jnp.exp(peak - largest), "src")
    return largest + jnp.log(summed)


def send_buffer(corrected, raw_mass, shard_counts, width):
    blocks = lax.axis_size("src")
    mine = lax.axis_index("src")
    starts = jnp.cumsum(shard_counts) - shard_counts
    wanted = (
        jnp.arange(blocks, dtype=jnp.int32)[:, None] * S_DEV
        + jnp.arange(width, dtype=jnp.int32)[None, :]
    )
    local = wanted - starts[mine]
    valid = (local >= 0) & (local < shard_counts[mine])
    safe = jnp.clip(local, 0, CAP - 1)
    feats = jnp.take(corrected, safe.reshape(-1), axis=1).reshape(corrected.shape[0], blocks, width)
    feats = jnp.where(valid[None], feats, 0.0)
    masses = jnp.where(valid, jnp.take(raw_mass, safe.reshape(-1)).reshape(blocks, width), 0.0)[
        None
    ]
    return (feats, masses)


def on_device(
    src_features, src_mass, section_ids, shard_counts, section_offsets, tgt_features, tgt_mass
):
    onehot = (section_ids[None, :] == jnp.arange(SECTIONS, dtype=jnp.int32)[:, None]).astype(
        jnp.float32
    )
    corrected = src_features - jnp.dot(
        section_offsets, onehot, precision=HIGH, preferred_element_type=jnp.float32
    )
    feats, masses = send_buffer(corrected, src_mass, shard_counts, S_DEV)
    got = (
        lax.all_to_all(feats, "src", split_axis=1, concat_axis=1, tiled=True),
        lax.all_to_all(masses, "src", split_axis=1, concat_axis=1, tiled=True),
    )
    src_x = jnp.sum(got[0], axis=1)
    src_m = jnp.sum(got[1], axis=1)[0]
    ratio = lax.axis_size("tgt") // lax.axis_size("src")
    piece = S_DEV // ratio
    column = lax.axis_index("tgt")
    root = column // ratio
    start = column % ratio * piece
    own_x = lax.dynamic_slice_in_dim(src_x, start, piece, 1)
    own_m = lax.dynamic_slice_in_dim(src_m, start, piece, 0)
    self_x, self_m = (from_root(own_x, "src", root), from_root(own_m, "src", root))
    log_src = jnp.log(src_m)
    log_self = jnp.log(self_m)
    log_tgt = jnp.log(tgt_mass)
    sq_src = jnp.sum(src_x * src_x, axis=0)
    sq_self = jnp.sum(self_x * self_x, axis=0)
    sq_tgt = jnp.sum(tgt_features * tgt_features, axis=0)
    src_pot = jnp.zeros((S_DEV,), jnp.float32)
    tgt_pot = jnp.zeros((tgt_features.shape[1],), jnp.float32)
    self_pot = jnp.zeros((S_DEV,), jnp.float32)
    for step in range(ITERS):
        column_pot = from_root(lax.dynamic_slice_in_dim(self_pot, start, piece, 0), "src", root)
        f_peak, f_total = row_partials(src_x, sq_src, tgt_features, sq_tgt, log_tgt + tgt_pot / EPS)
        p_peak, p_total = row_partials(src_x, sq_src, self_x, sq_self, log_self + column_pot / EPS)
        lse_f, lse_p = reduce_rows(f_peak, f_total, p_peak, p_total)
        src_pot = -TAU * EPS * lse_f
        self_pot = 0.5 * (self_pot + -TAU * EPS * lse_p)
        g_peak, g_total = column_partials(
            src_x, sq_src, tgt_features, sq_tgt, log_src + src_pot / EPS
        )
        tgt_pot = -TAU * EPS * reduce_columns(g_peak, g_total)
    return (src_pot, tgt_pot, self_pot)


def solution(mesh):
    return jax.shard_map(
        on_device,
        mesh=mesh,
        in_specs=(P(None, "src"), P("src"), P("src"), P(), P(), P(None, "tgt"), P("tgt")),
        out_specs=(P("src"), P("tgt"), P("src")),
        check_vma=False,
    )
```

profile of v0, /device:TPU:1, one launch (start us, length us, event | category | flops | bytes accessed | tf_op | source)
XLA Modules:
  0.0 1539.7 jit_solution(17824634526186194368)
XLA Ops:
  11.5 90.5 %gather_fusion = f32[16384]{0:T(1024)S(1)} fusion(f32[8192]{0:T(1024)S(1)} %copy-done, s32[16384]{0:T(1024)S(1)} %broadcast_clamp_fusion), kind=kCustom, calls=%fused_computation | custom fusion | bytes 196608 | tf_op jit(solution)/shard_map/jit(_take)/gather | solution.py:92
  115.6 56.6 %gather_fusion.1 = f32[16384,50]{1,0:T(8,128)} fusion(f32[50,8192]{0,1:T(8,128)} %copy.21, s32[16384]{0:T(1024)S(1)} %broadcast_clamp_fusion), kind=kCustom, calls=%fused_computation.1 | custom fusion | bytes 6619136 | tf_op jit(solution)/shard_map/jit(_take)/gather | solution.py:90
  172.2 6.7 copy.22
  188.9 42.7 %psum.100 = f32[512]{0:T(512)S(1)} all-reduce(f32[512]{0:T(512)S(1)} %dynamic-slice_select_fusion.3), channel_id=1, replica_groups=mesh['src'=4,'tgt'=32] {'src'}, use_global_device_ids=true, to_apply=%region_41.42 | all-reduce | flops 512 | bytes 4096 | tf_op jit(solution)/shard_map/psum | solution.py:19
  236.6 24.2 %while.111 = (s32[]{:T(128)}, f32[8,512]{1,0:T(8,128)S(1)}, f32[8,512]{1,0:T(8,128)S(1)}, f32[1024]{0:T(1024)S(1)}, f32[8,512]{1,0:T(8,128)S(1)}, /*index=5*/f32...) while((s32[]{:T(128)}, f32[8,512]{1,0:T(8,128)S(1)}, ...), condition=%wide.region_8.9_spmd, body=%wide.region_5.8_spmd.sunk | while | flops 318766080 | bytes 4567157 | solution.py:45
  260.8 14.7 all-reduce.10.cloned.1.call-done
  277.8 12.4 while.114
  290.2 156.3 %all-reduce.5 = (f32[4096]{0:T(1024)S(1)}, f32[4096]{0:T(1024)S(1)}) all-reduce(f32[4096]{0:T(1024)S(1)} %bitcast.243, f32[4096]{0:T(1024)S(1)} %bitcast.245), channel_id=1, replica_groups=mesh['src'=4,'tgt'=32] {'tgt'}, use_global_device_ids=true, to_apply=%region_9.10 | all-reduce | flops 8192 | bytes 65536 | tf_op jit(solution)/shard_map/pmax | solution.py:66
  446.5 149.8 %all-reduce.2 = (f32[4096]{0:T(1024)S(1)}, f32[4096]{0:T(1024)S(1)}) all-reduce(f32[4096]{0:T(1024)S(1)} %get-tuple-element.822, f32[4096]{0:T(1024)S(1)} %get-tuple-element.821), channel_id=1, replica_groups=mesh['src'=4,'tgt'=32] {'tgt'}, use_global_device_ids=true, to_apply=%region_10.11 | all-reduce | flops 8192 | bytes 65536 | tf_op jit(solution)/shard_map/psum | solution.py:67
  596.4 20.8 %while.117 = (s32[]{:T(128)}, f32[1024]{0:T(1024)S(1)}, f32[1024]{0:T(1024)S(1)}, f32[8,512]{1,0:T(8,128)S(1)}, f32[8,512]{1,0:T(8,128)S(1)}, /*index=5*/f32[102...) while((s32[]{:T(128)}, f32[1024]{0:T(1024)S(1)}, ...), condition=%wide.region_14.15_spmd.clone, body=%wide.region_11.14_spmd.clone.sunk | while | flops 318772224 | bytes 4608120 | solution.py:61
  617.2 60.2 %pmax.64 = f32[1024]{0:T(1024)S(1)} all-reduce(f32[1024]{0:T(1024)S(1)} %get-tuple-element.392), channel_id=1, replica_groups=mesh['src'=4,'tgt'=32] {'src'}, use_global_device_ids=true, to_apply=%region_15.16 | all-reduce | flops 1024 | bytes 8192 | tf_op jit(solution)/shard_map/pmax | solution.py:74
  683.4 12.4 while.115
  695.8 24.1 %while.112 = (s32[]{:T(128)}, f32[8,512]{1,0:T(8,128)S(1)}, f32[8,512]{1,0:T(8,128)S(1)}, f32[1024]{0:T(1024)S(1)}, f32[8,512]{1,0:T(8,128)S(1)}, /*index=5*/f32...) while((s32[]{:T(128)}, f32[8,512]{1,0:T(8,128)S(1)}, ...), condition=%wide.region_20.21_spmd, body=%wide.region_17.20_spmd.sunk | while | flops 318766080 | bytes 4567157 | solution.py:45
  720.0 149.0 %all-reduce.4 = (f32[4096]{0:T(1024)S(1)}, f32[4096]{0:T(1024)S(1)}) all-reduce(f32[4096]{0:T(1024)S(1)} %bitcast.239, f32[4096]{0:T(1024)S(1)} %bitcast.237), channel_id=1, replica_groups=mesh['src'=4,'tgt'=32] {'tgt'}, use_global_device_ids=true, to_apply=%region_21.22 | all-reduce | flops 8192 | bytes 65536 | tf_op jit(solution)/shard_map/pmax | solution.py:66
  869.1 149.7 %all-reduce.1 = (f32[4096]{0:T(1024)S(1)}, f32[4096]{0:T(1024)S(1)}) all-reduce(f32[4096]{0:T(1024)S(1)} %exponential_multiply_fusion.4, f32[4096]{0:T(1024)S(1)} %exponential_multiply_fusion.1), channel_id=1, replica_groups=mesh['src'=4,'tgt'=32] {'tgt'}, use_global_device_ids=true, to_apply=%region_22.23 | all-reduce | flops 8192 | bytes 65536 | tf_op jit(solution)/shard_map/psum | solution.py:67
  1018.9 20.9 %while.118 = (s32[]{:T(128)}, f32[1024]{0:T(1024)S(1)}, f32[1024]{0:T(1024)S(1)}, f32[8,512]{1,0:T(8,128)S(1)}, f32[8,512]{1,0:T(8,128)S(1)}, /*index=5*/f32[102...) while((s32[]{:T(128)}, f32[1024]{0:T(1024)S(1)}, ...), condition=%wide.region_26.27_spmd.clone, body=%wide.region_23.26_spmd.clone.sunk | while | flops 318772224 | bytes 4608120 | solution.py:61
  1039.7 61.1 %pmax.66 = f32[1024]{0:T(1024)S(1)} all-reduce(f32[1024]{0:T(1024)S(1)} %get-tuple-element.396), channel_id=1, replica_groups=mesh['src'=4,'tgt'=32] {'src'}, use_global_device_ids=true, to_apply=%region_27.28 | all-reduce | flops 1024 | bytes 8192 | tf_op jit(solution)/shard_map/pmax | solution.py:74
  1100.8 6.0 all-reduce.6
  1106.8 12.4 while.116
  1119.3 24.1 %while.113 = (s32[]{:T(128)}, f32[8,512]{1,0:T(8,128)S(1)}, f32[8,512]{1,0:T(8,128)S(1)}, f32[1024]{0:T(1024)S(1)}, f32[8,512]{1,0:T(8,128)S(1)}, /*index=5*/f32...) while((s32[]{:T(128)}, f32[8,512]{1,0:T(8,128)S(1)}, ...), condition=%wide.region_32.33_spmd, body=%wide.region_29.32_spmd.sunk | while | flops 318766080 | bytes 4567157 | solution.py:45
  1143.5 149.1 %all-reduce.3 = (f32[4096]{0:T(1024)S(1)}, f32[4096]{0:T(1024)S(1)}) all-reduce(f32[4096]{0:T(1024)S(1)} %bitcast.241, f32[4096]{0:T(1024)S(1)} %bitcast.235), channel_id=1, replica_groups=mesh['src'=4,'tgt'=32] {'tgt'}, use_global_device_ids=true, to_apply=%region_33.34 | all-reduce | flops 8192 | bytes 65536 | tf_op jit(solution)/shard_map/pmax | solution.py:66
  1292.6 149.0 %all-reduce = (f32[4096]{0:T(1024)S(1)}, f32[4096]{0:T(1024)S(1)}) all-reduce(f32[4096]{0:T(1024)S(1)} %exponential_multiply_fusion.3, f32[4096]{0:T(1024)S(1)} %exponential_multiply_fusion), channel_id=1, replica_groups=mesh['src'=4,'tgt'=32] {'tgt'}, use_global_device_ids=true, to_apply=%region_34.35 | all-reduce | flops 8192 | bytes 65536 | tf_op jit(solution)/shard_map/psum | solution.py:67
  1442.8 20.9 %while.119 = (s32[]{:T(128)}, f32[1024]{0:T(1024)S(1)}, f32[1024]{0:T(1024)S(1)}, f32[8,512]{1,0:T(8,128)S(1)}, f32[8,512]{1,0:T(8,128)S(1)}, /*index=5*/f32[102...) while((s32[]{:T(128)}, f32[1024]{0:T(1024)S(1)}, ...), condition=%wide.region_38.39_spmd.clone, body=%wide.region_35.38_spmd.clone.sunk | while | flops 318772224 | bytes 4608120 | solution.py:61
  1463.7 62.8 %pmax.68 = f32[1024]{0:T(1024)S(1)} all-reduce(f32[1024]{0:T(1024)S(1)} %get-tuple-element.400), channel_id=1, replica_groups=mesh['src'=4,'tgt'=32] {'src'}, use_global_device_ids=true, to_apply=%region_39.40 | all-reduce | flops 1024 | bytes 8192 | tf_op jit(solution)/shard_map/pmax | solution.py:74
  (483 shorter events, 217.7 us)
Async XLA Ops:
  7.2 4.3 copy-start
  11.4 99.0 %copy-start.3 = (s32[8192]{0:T(1024)S(1)}, s32[8192]{0:T(1024)}, u32[]{:S(2)}) copy-start(s32[8192]{0:T(1024)} %param.27) | copy-start | bytes 98308
  11.4 99.0 %copy-start.4 = (f32[50,32]{0,1:T(8,128)S(1)}, f32[50,32]{0,1:T(8,128)}, u32[]{:S(2)}) copy-start(f32[50,32]{0,1:T(8,128)} %param.29) | copy-start | bytes 19204
  104.3 79.3 %all-to-all-start = ((f32[1,4,4096]{2,0,1:T(1,128)}), f32[1,4,4096]{2,0,1:T(1,128)S(1)}, u32[]{:S(2)}, u32[]{:S(2)}) async-start(f32[1,4,4096]{2,0,1:T(1,128)} %and_select_fusion.1), calls=%async_computation | async-start | bytes 131072 | tf_op jit(solution)/shard_map/all_to_all | solution.py:110
  183.5 5.1 copy-start.2
  183.5 5.1 copy-start.1
  183.6 48.0 %all-to-all-start.1 = ((f32[50,4,4096]{2,0,1:T(8,128)}), f32[50,4,4096]{2,0,1:T(8,128)}, u32[]{:S(2)}, u32[]{:S(2)}) async-start(f32[50,4,4096]{2,0,1:T(8,128)} %select_select_fusion), calls=%async_computation.1 | async-start | bytes 7340032 | tf_op jit(solution)/shard_map/all_to_all | solution.py:109
  188.5 87.1 %all-reduce.10.cloned.1.call-start = ((), (), s32[]{:S(2)}) async-start(), calls=%async_computation.2 | async-start | bytes 524288 | tf_op jit(solution)/shard_map/psum | solution.py:19
Sparse Core Ops, SparseCore 0:
  236.0 39.4 all-reduce.9
where the time goes:
time: 1540 us
  blocking collectives  1150 us (75%)
  local copies, waits for them, and re-layouts  167 us (11%)
  matrix products  140 us (9%)
  other arithmetic  43.2 us (3%)
    pmax x3, blocking collectives, reduce_rows(): peaks = lax.pmax((f_peak, p_peak), 'tgt')  454 us
    psum x3, blocking collectives, reduce_rows(): lax.psum((f_total * jnp.exp(f_peak - peaks[0]), p_total * jnp.exp(p_peak...  448 us
    pmax x3, blocking collectives, reduce_columns(): largest = lax.pmax(peak, 'src')  184 us
    dot_general x72, matrix products, tile_cost(): lax.dot_general(xa, xb, (((0,), (0,)), ((), ())), precision=HIGH, preferr...  137 us
    gather x1, local copies, waits for them, and re-layouts, send_buffer(): jnp.take(raw_mass, safe.reshape(-1)).reshape(blocks, width)  90.5 us
    gather x2, local copies, waits for them, and re-layouts, send_buffer(): jnp.take(corrected, safe.reshape(-1), axis=1)  63.3 us
    psum x1, blocking collectives, from_root(): return lax.psum(kept, axis)  42.7 us
  transfers between devices with their start and end apart: 3, of which 1 were waited for; matrix products, arithmetic and copies ran while one was open for 6% of the time, Pallas kernels for 0%

commit v1 on v0

v1 whole, which is shorter than its diff:
```python
import jax
import jax.numpy as jnp
from jax import lax
from jax.experimental import pallas as pl
from jax.experimental.pallas import tpu as pltpu
from jax.sharding import PartitionSpec as P

COMPONENTS = 50
ROWS = 56
SECTIONS = 32
ITERS = 3
CAP = 8192
GROUP = 2048
HALF = 1024
SPAN = GROUP + 128
LEAD = GROUP
WIDTH = LEAD + CAP + SPAN

EPS = 0.05
TAU = 1.0 / (1.0 + EPS)
LOG2E = 1.4426950408889634
SCALE = LOG2E / EPS

F32 = jnp.float32
BF16 = jnp.bfloat16
MESH = pl.DeviceIdType.MESH
TILE = 256
CHUNK = 512


def place():
    src, tgt = lax.axis_index("src"), lax.axis_index("tgt")
    z, rest = lax.div(tgt, 8), lax.rem(tgt, 8)
    return (
        lax.div(src, 2),
        lax.rem(src, 2),
        lax.div(z, 2),
        lax.rem(z, 2),
        lax.div(rest, 2),
        lax.rem(rest, 2),
    )


def device(x_lo, core, z_hi, z_lo, y, x_hi):
    return (x_lo * 2 + core, (z_hi * 2 + z_lo) * 8 + y * 2 + x_hi)


def pieces(value):
    high = value.astype(BF16)
    rest = value - high.astype(F32)
    middle = rest.astype(BF16)
    return high, middle, (rest - middle.astype(F32)).astype(BF16)


def relay_kernel(counts_ref, feats_ref, mass_ref, ids_ref, offsets_ref, out_ref, held):
    x_lo, core, z_hi, z_lo, y, x_hi = place()
    mine = x_lo * 2 + core
    start = jnp.int32(0)
    for k in range(3):
        start = start + jnp.where(k < mine, counts_ref[k], 0)
    count = counts_ref[mine]
    three = jnp.concatenate([p.astype(F32) for p in pieces(offsets_ref[...])], axis=1).astype(BF16)
    for at in range(0, CAP, 1024):
        ids = ids_ref[:, at : at + 1024]
        section = lax.rem(lax.broadcasted_iota(jnp.int32, (3 * SECTIONS, 1024), 0), SECTIONS)
        onehot = jnp.where(section == ids, 1.0, 0.0).astype(BF16)
        shift = jnp.dot(three, onehot, preferred_element_type=F32)
        to = slice(LEAD + at, LEAD + at + 1024)
        held[48:ROWS, to] = jnp.zeros((ROWS - 48, 1024), F32)
        held[0:COMPONENTS, to] = feats_ref[:, at : at + 1024] - shift
        held[COMPONENTS : COMPONENTS + 1, to] = mass_ref[:, at : at + 1024]
    lane = lax.broadcasted_iota(jnp.int32, (ROWS, 128), 1)

    def contribute(index, carry):
        to_x = lax.rem(x_lo + lax.div(index, 2), 2)
        to_core = lax.rem(core + lax.rem(index, 2), 2)
        base = (to_x * 2 + to_core) * (2 * GROUP) + z_lo * GROUP - start
        at = jnp.clip(base, -LEAD, CAP) + LEAD
        aligned = pl.multiple_of(lax.div(at, 128) * 128, 128)
        off = lax.rem(at, 128)
        turn = lax.rem(128 - off, 128)
        before = pltpu.roll(held[:, pl.ds(aligned, 128)], turn, 1)
        for t in range(GROUP // 128):
            after = pltpu.roll(
                held[:, pl.ds(pl.multiple_of(aligned + (t + 1) * 128, 128), 128)], turn, 1
            )
            value = jnp.where(lane < 128 - off, before, after)
            local = lane + (base + t * 128)
            value = jnp.where((local >= 0) & (local < count), value, 0.0)
            out_ref[index, :, t * 128 : (t + 1) * 128] = value
            before = after
        return carry

    lax.fori_loop(0, 4, contribute, 0)


def log_sum(parts):
    peak = jnp.max(parts, axis=0)
    return peak + jnp.log2(jnp.sum(jnp.exp2(parts - peak[None]), axis=0))


def lse_pass(lhs, rhs, bufs, count, put):
    tiles = GROUP // TILE
    chunk = min(CHUNK, count)

    def both(j_made, made, j_used, used, peak):
        columns = rhs[:, pl.ds(pl.multiple_of(j_made * TILE, TILE), TILE)]
        top, total = None, None
        for at in range(0, count, chunk):
            s = jnp.dot(lhs[at : at + chunk, :], columns, preferred_element_type=F32)
            made[at : at + chunk, :] = s
            here = jnp.max(s, axis=0, keepdims=True)
            top = here if top is None else jnp.maximum(top, here)
            if peak is not None:
                e = jnp.exp2(used[at : at + chunk, :] - peak)
                part = jnp.sum(e, axis=0, keepdims=True)
                total = part if total is None else total + part
        if peak is not None:
            put(j_used, peak + jnp.log2(total))
        return top

    first = both(0, bufs[0], None, None, None)

    def body(pair, peak):
        j = 2 * pair
        peak = both(j + 1, bufs[1], j, bufs[0], peak)
        return both(lax.rem(j + 2, tiles), bufs[0], j + 1, bufs[1], peak)

    lax.fori_loop(0, tiles // 2, body, first)


def to_rows(ref, row):
    for r in range(row.shape[1] // 128):
        ref[r : r + 1, :] = row[:, r * 128 : (r + 1) * 128]


def set_weights(lhs, fixed, weight):
    rows = weight.shape[0]
    parts = [p.astype(F32) for p in pieces(weight)]
    stacked = jnp.concatenate(parts + [jnp.zeros((128 - 3 * rows, 128), F32)], axis=0)
    turned = stacked.T
    lane = lax.rem(lax.broadcasted_iota(jnp.int32, (128, 128), 1), rows)
    for c in range(rows):
        at = slice(c * 128, (c + 1) * 128)
        lhs[at, 128:256] = jnp.where(lane == c, turned, 0.0).astype(BF16) + fixed[at, :]


def set_left(lhs, fixed, one, two, three):
    zero = jnp.zeros((64, 128), F32)
    for c in range(one.shape[1] // 128):
        at = slice(c * 128, (c + 1) * 128)
        first = jnp.concatenate([one[:, at].astype(F32), two[:, at].astype(F32)], axis=0)
        second = jnp.concatenate([zero, three[:, at].astype(F32)], axis=0)
        lhs[at, 0:128] = first.T.astype(BF16)
        fixed[at, :] = second.T.astype(BF16)


def set_right(rhs, one, two, three):
    rhs[0:64, :] = one
    rhs[64:128, :] = two
    row = lax.broadcasted_iota(jnp.int32, (64, GROUP), 0)
    rhs[128:192, :] = jnp.where(row < 48, 1.0, 0.0).astype(BF16)
    rhs[192:256, :] = three


def padded(cells, centre):
    row = lax.broadcasted_iota(jnp.int32, cells.shape, 0)
    kept = jnp.where(row < COMPONENTS, cells - centre, 0.0)
    return jnp.concatenate([kept, jnp.zeros((64 - ROWS, cells.shape[1]), F32)], axis=0)


def sinkhorn_kernel(
    con_ref, tgt_ref, mass_ref,
    src_out, tgt_out, self_out,
    from_own, from_opp, opp, landed, ybuf, xfull, sbuf,
    lhs_x, lhs_y, lhs_s, fix_x, fix_y, fix_s, rhs_x, rhs_y, buf_a, buf_b,
    sq_x, sq_y, sq_s, log_x, log_y, log_s, pot_p, pot_s, wide,
    fy, fz, py, pz, gb, pots, fin,
    relay_send, relay_recv, opp_send, opp_recv, own_sem, tgt_sem, self_sem, local_sem,
    fy_send, fy_recv, fz_send, fz_recv, py_send, py_recv, pz_send, pz_recv,
    gb_send, gb_recv, pot_send, pot_recv, fin_send, fin_recv,
):
    x_lo, core, z_hi, z_lo, y, x_hi = place()
    sibling = device(x_lo, 1 - core, z_hi, z_lo, y, x_hi)
    twin = device(x_lo, core, z_hi, 1 - z_lo, y, x_hi)
    across = device(1 - x_lo, core, z_hi, z_lo, y, 1 - x_hi)
    straight = lax.rem(x_lo + core, 2)
    opposite = device(1 - x_lo, core, z_hi, z_lo, y, lax.rem(x_hi + straight, 2))
    y_hi, y_lo = lax.div(y, 2), lax.rem(y, 2)
    partner = device(
        lax.rem(x_lo + y_hi, 2), lax.rem(core + y_lo, 2), z_hi, lax.rem(z_lo + z_hi, 2), y, x_hi
    )
    alone = (y + z_hi) == 0
    g = x_lo * 4 + core * 2 + z_lo
    zx = z_hi * 2 + x_hi

    def y_peer(k):
        return device(x_lo, core, z_hi, z_lo, k, x_hi)

    def zx_peer(k):
        return device(x_lo, core, lax.div(k, 2), z_lo, y, lax.rem(k, 2))

    def g_peer(k):
        return device(lax.div(k, 4), lax.rem(lax.div(k, 2), 2), z_hi, lax.rem(k, 2), y, x_hi)

    y_others = [lax.rem(y + d, 4) for d in range(1, 4)]
    zx_others = [lax.rem(zx + d, 4) for d in range(1, 4)]
    g_others = [lax.rem(g + d, 8) for d in range(1, 8)]

    barrier = pltpu.get_barrier_semaphore()
    peers = [y_peer(k) for k in y_others] + [zx_peer(k) for k in zx_others]
    peers += [g_peer(k) for k in g_others] + [across]
    for peer in peers:
        pl.semaphore_signal(barrier, inc=1, device_id=peer, device_id_type=MESH)

    ybuf[z_lo, 48:ROWS, :] = jnp.zeros((ROWS - 48, HALF), F32)
    ybuf[z_lo, 0:COMPONENTS, :] = tgt_ref[...]
    ybuf[z_lo, COMPONENTS : COMPONENTS + 1, :] = mass_ref[...]

    pl.semaphore_wait(barrier, len(peers))

    def remote(src, dst, send, recv, to):
        return pltpu.make_async_remote_copy(
            src_ref=src, dst_ref=dst, send_sem=send, recv_sem=recv, device_id=to,
            device_id_type=MESH,
        )

    parts = [slice(c * 512, (c + 1) * 512) for c in range(4)]
    relays = [
        remote(con_ref.at[3, :, s], from_opp.at[:, s], relay_send.at[c], relay_recv.at[c], sibling)
        for c, s in enumerate(parts)
    ]
    for copy in relays:
        copy.start()
    own = remote(con_ref.at[1], from_own, own_sem.at[0], own_sem.at[1], sibling)
    own.start()
    tgt = remote(ybuf.at[z_lo], ybuf.at[z_lo], tgt_sem.at[0], tgt_sem.at[1], twin)
    tgt.start()
    onward = [
        remote(opp.at[:, s], landed.at[:, s], opp_send.at[c], opp_recv.at[c], opposite)
        for c, s in enumerate(parts)
    ]
    for c, s in enumerate(parts):
        relays[c].wait_recv()
        opp[:, s] = con_ref[2, :, s] + from_opp[:, s]
        onward[c].start()

    remote(ybuf.at[1 - z_lo], ybuf.at[1 - z_lo], tgt_sem.at[0], tgt_sem.at[1], twin).wait_recv()
    cells = jnp.concatenate([ybuf[0], ybuf[1]], axis=1)
    centre = jnp.sum(cells, axis=1, keepdims=True) * (1.0 / GROUP)
    kept = padded(cells, centre)
    to_rows(sq_y, jnp.sum(kept * kept, axis=0, keepdims=True) * SCALE)
    to_rows(log_y, jnp.log2(cells[COMPONENTS : COMPONENTS + 1, :]))
    high, middle, unused = pieces(kept)
    set_left(lhs_y, fix_y, high, high, middle)
    set_right(rhs_y, high, high, middle)
    set_weights(lhs_y, fix_y, log_y[...] - sq_y[...])

    own.wait_recv()
    for copy in onward:
        copy.wait_recv()
    cells = con_ref[0] + from_own[...] + landed[...]
    xfull[...] = cells
    half = pl.ds(pl.multiple_of(x_hi * HALF, HALF), HALF)
    shared = remote(xfull.at[:, half], sbuf, self_sem.at[0], self_sem.at[1], partner)
    kept_here = pltpu.make_async_copy(xfull.at[:, half], sbuf, local_sem)

    @pl.when(alone)
    def _():
        kept_here.start()

    @pl.when(jnp.logical_not(alone))
    def _():
        shared.start()

    kept = padded(cells, centre)
    to_rows(sq_x, jnp.sum(kept * kept, axis=0, keepdims=True) * SCALE)
    to_rows(log_x, jnp.log2(cells[COMPONENTS : COMPONENTS + 1, :]))
    high, middle, unused = pieces(kept * (2.0 * SCALE))
    set_right(rhs_x, high, middle, high)
    set_left(lhs_x, fix_x, high, middle, high)
    for copy in relays + onward + [own, tgt]:
        copy.wait_send()

    pot_p[...] = jnp.zeros_like(pot_p)
    pot_s[...] = jnp.zeros_like(pot_s)

    def put_wide(j, value):
        wide[pl.ds(2 * j, 1), :] = value[:, 0:128]
        wide[pl.ds(2 * j + 1, 1), :] = value[:, 128:256]

    def spread(box, it, me, others, peer, send, recv):
        for k in others:
            remote(box.at[it, me], box.at[it, me], send.at[it, k], recv.at[it, me], peer(k)).start()

    def collect(box, it, me, others, peer, send, recv):
        for k in others:
            remote(box.at[it, k], box.at[it, k], send.at[it, k], recv.at[it, k], peer(k)).wait_recv()
        for k in others:
            remote(box.at[it, me], box.at[it, me], send.at[it, k], recv.at[it, me], peer(k)).wait_send()
        return log_sum(box[it])

    bufs = (buf_a, buf_b)
    half_rows = pl.ds(pl.multiple_of(x_hi * 8, 8), 8)

    def iteration(it, carry):
        lse_pass(lhs_y, rhs_x, bufs, GROUP, put_wide)
        fy[it, y] = wide[...] - sq_x[...]
        spread(fy, it, y, y_others, y_peer, fy_send, fy_recv)

        @pl.when(it == 0)
        def _():
            @pl.when(alone)
            def _():
                kept_here.wait()

            @pl.when(jnp.logical_not(alone))
            def _():
                shared.wait_recv()
                shared.wait_send()

            got = sbuf[...]
            columns = padded(got, centre)
            to_rows(sq_s, jnp.sum(columns * columns, axis=0, keepdims=True) * SCALE)
            to_rows(log_s, jnp.log2(got[COMPONENTS : COMPONENTS + 1, :]))
            upper, lower, unused = pieces(columns)
            set_left(lhs_s, fix_s, upper, upper, lower)

        @pl.when(it > 0)
        def _():
            last = it - 1

            @pl.when(alone)
            def _():
                pot_s[...] = pot_p[half_rows, :]

            @pl.when(jnp.logical_not(alone))
            def _():
                moved = remote(
                    pots.at[0, last], pots.at[1, last], pot_send.at[last], pot_recv.at[last],
                    partner,
                )
                moved.wait_recv()
                moved.wait_send()
                pot_s[...] = pots[1, last]

        set_weights(lhs_s, fix_s, log_s[...] + pot_s[...] - sq_s[...])
        lse_pass(lhs_s, rhs_x, bufs, HALF, put_wide)
        py[it, y] = wide[...] - sq_x[...]
        spread(py, it, y, y_others, y_peer, py_send, py_recv)

        fz[it, zx] = collect(fy, it, y, y_others, y_peer, fy_send, fy_recv)
        spread(fz, it, zx, zx_others, zx_peer, fz_send, fz_recv)
        pz[it, zx] = collect(py, it, y, y_others, y_peer, py_send, py_recv)
        spread(pz, it, zx, zx_others, zx_peer, pz_send, pz_recv)
        pot_f = -TAU * collect(fz, it, zx, zx_others, zx_peer, fz_send, fz_recv)
        set_weights(lhs_x, fix_x, log_x[...] + pot_f - sq_x[...])

        @pl.when(it == ITERS - 1)
        def _():
            fin[0, z_lo] = pot_f * (1.0 / SCALE)
            remote(
                fin.at[0, z_lo], fin.at[0, z_lo], fin_send.at[0], fin_recv.at[0], twin
            ).start()

        lse_pass(lhs_x, rhs_y, bufs, GROUP, put_wide)
        gb[it, g] = wide[...] - sq_y[...]
        spread(gb, it, g, g_others, g_peer, gb_send, gb_recv)

        new_p = -TAU * collect(pz, it, zx, zx_others, zx_peer, pz_send, pz_recv)
        pot_p[...] = 0.5 * (pot_p[...] + new_p)

        @pl.when((it < ITERS - 1) & jnp.logical_not(alone))
        def _():
            pots[0, it] = pot_p[half_rows, :]
            remote(
                pots.at[0, it], pots.at[1, it], pot_send.at[it], pot_recv.at[it], partner
            ).start()

        @pl.when(it == ITERS - 1)
        def _():
            fin[1, z_lo] = pot_p[...] * (1.0 / SCALE)
            remote(
                fin.at[1, z_lo], fin.at[1, z_lo], fin_send.at[1], fin_recv.at[1], twin
            ).start()

        pot_g = -TAU * collect(gb, it, g, g_others, g_peer, gb_send, gb_recv)
        wide[...] = pot_g

        @pl.when(it < ITERS - 1)
        def _():
            set_weights(lhs_y, fix_y, log_y[...] + pot_g - sq_y[...])

        return carry

    lax.fori_loop(0, ITERS, iteration, 0)

    tgt_out[...] = wide[pl.ds(pl.multiple_of(z_lo * 8, 8), 8), :] * (1.0 / SCALE)
    for kind in range(2):
        remote(
            fin.at[kind, 1 - z_lo], fin.at[kind, 1 - z_lo], fin_send.at[kind], fin_recv.at[kind],
            twin,
        ).wait_recv()
        remote(
            fin.at[kind, z_lo], fin.at[kind, z_lo], fin_send.at[kind], fin_recv.at[kind], twin
        ).wait_send()
    src_out[0:16, :] = fin[0, 0]
    src_out[16:32, :] = fin[0, 1]
    self_out[0:16, :] = fin[1, 0]
    self_out[16:32, :] = fin[1, 1]


def on_device(
    src_features, src_mass, section_ids, shard_counts, section_offsets, tgt_features, tgt_mass
):
    vmem = pl.BlockSpec(memory_space=pltpu.VMEM)
    contributions = pl.pallas_call(
        relay_kernel,
        out_shape=jax.ShapeDtypeStruct((4, ROWS, GROUP), F32),
        in_specs=[pl.BlockSpec(memory_space=pltpu.SMEM)] + [vmem] * 4,
        out_specs=vmem,
        scratch_shapes=[pltpu.VMEM((ROWS, WIDTH), F32)],
        compiler_params=pltpu.CompilerParams(vmem_limit_bytes=32 * 1024 * 1024),
    )(
        shard_counts,
        src_features,
        src_mass.reshape(1, CAP),
        section_ids.reshape(1, CAP),
        section_offsets,
    )
    V, D = pltpu.VMEM, pltpu.SemaphoreType.DMA
    rows16, rows8 = (16, 128), (8, 128)
    outs = pl.pallas_call(
        sinkhorn_kernel,
        out_shape=(
            jax.ShapeDtypeStruct((32, 128), F32),
            jax.ShapeDtypeStruct((8, 128), F32),
            jax.ShapeDtypeStruct((32, 128), F32),
        ),
        in_specs=[vmem] * 3,
        out_specs=(vmem, vmem, vmem),
        scratch_shapes=[
            V((ROWS, GROUP), F32), V((ROWS, GROUP), F32), V((ROWS, GROUP), F32),
            V((ROWS, GROUP), F32), V((2, ROWS, HALF), F32), V((ROWS, GROUP), F32),
            V((ROWS, HALF), F32),
            V((GROUP, 256), BF16), V((GROUP, 256), BF16), V((HALF, 256), BF16),
            V((GROUP, 128), BF16), V((GROUP, 128), BF16), V((HALF, 128), BF16),
            V((256, GROUP), BF16), V((256, GROUP), BF16),
            V((GROUP, TILE), F32), V((GROUP, TILE), F32),
            V(rows16, F32), V(rows16, F32), V(rows8, F32),
            V(rows16, F32), V(rows16, F32), V(rows8, F32),
            V(rows16, F32), V(rows8, F32), V(rows16, F32),
            V((ITERS, 4) + rows16, F32), V((ITERS, 4) + rows16, F32),
            V((ITERS, 4) + rows16, F32), V((ITERS, 4) + rows16, F32),
            V((ITERS, 8) + rows16, F32), V((2, ITERS - 1) + rows8, F32),
            V((2, 2) + rows16, F32),
            D((4,)), D((4,)), D((4,)), D((4,)), D((2,)), D((2,)), D((2,)), D,
            D((ITERS, 4)), D((ITERS, 4)), D((ITERS, 4)), D((ITERS, 4)),
            D((ITERS, 4)), D((ITERS, 4)), D((ITERS, 4)), D((ITERS, 4)),
            D((ITERS, 8)), D((ITERS, 8)), D((ITERS,)), D((ITERS,)), D((2,)), D((2,)),
        ],
        compiler_params=pltpu.CompilerParams(
            collective_id=0, has_side_effects=True, vmem_limit_bytes=48 * 1024 * 1024
        ),
    )(contributions, tgt_features, tgt_mass.reshape(1, HALF))
    return (outs[0].reshape(2 * GROUP), outs[1].reshape(HALF), outs[2].reshape(2 * GROUP))


def solution(mesh):
    return jax.shard_map(
        on_device,
        mesh=mesh,
        in_specs=(P(None, "src"), P("src"), P("src"), P(), P(), P(None, "tgt"), P("tgt")),
        out_specs=(P("src"), P("tgt"), P("src")),
        check_vma=False,
    )
```

time: 1540 us -> 93.8 us (0.06)
  blocking collectives: 1150 us -> 0 us
  local copies, waits for them, and re-layouts: 167 us -> 6.29 us
  matrix products: 140 us -> 0 us
  Pallas kernels: 0 us -> 86.5 us
  other arithmetic: 43.2 us -> 0 us
    pmax x6 -> x0, blocking collectives: 639 us -> none  [the longest x3 454 us: reduce_rows(): peaks = lax.pmax((f_peak, p_peak), 'tgt')]
    psum x7 -> x0, blocking collectives: 509 us -> none  [the longest x3 448 us: reduce_rows(): lax.psum((f_total * jnp.exp(f_peak - peaks[0]), p_total * jnp.exp(p_peak...]
    gather x3 -> x0, local copies, waits for them, and re-layouts: 154 us -> none  [the longest x1 90.5 us: send_buffer(): jnp.take(raw_mass, safe.reshape(-1)).reshape(blocks, width)]
    dot_general x73 -> x0, matrix products: 140 us -> none  [the longest x72 137 us: tile_cost(): lax.dot_general(xa, xb, (((0,), (0,)), ((), ())), precision=HIGH, preferr...]
    pallas_call x0 -> x2, Pallas kernels: none -> 86.5 us  [the longest x1 84.6 us: on_device(): pl.pallas_call(sinkhorn_kernel, out_shape=(jax.ShapeDtypeStruct((32, 128)...]
    reduce_sum x77 -> x0, other arithmetic: 29.2 us -> none  [the longest x48 17.1 us: one(): return (peak, jnp.sum(jnp.exp(scores - peak[:, None]), axis=1))]
  transfers between devices with their start and end apart: 3 -> 0, of which waited for: 1 -> 0; matrix products, arithmetic and copies ran while one was open for 6% -> 0% of each run, Pallas kernels for 0% -> 0%
where the time goes in v1:
time: 93.8 us; the launch traced here: 93.5 us
  Pallas kernels  86.5 us (92%)
  local copies, waits for them, and re-layouts  6.29 us (7%)
    pallas_call x1, Pallas kernels, on_device(): pl.pallas_call(sinkhorn_kernel, out_shape=(jax.ShapeDtypeStruct((32, 128)...  84.6 us
    unnamed x16, local copies, waits for them, and re-layouts  6.29 us

profile of v1, /device:TPU:1, one launch (start us, length us, event | category | flops | bytes accessed | tf_op | source)
XLA Modules:
  0.0 93.5 jit_solution(2140288997495495895)
XLA Ops:
  0.6 0.8 copy.10.offsets_ref
  1.4 0.0 copy-start
  1.4 1.5 %copy-done = f32[50,8192]{1,0:T(8,128)S(1)} copy-done((f32[50,8192]{1,0:T(8,128)S(1)}, f32[50,8192]{1,0:T(8,128)}, u32[]{:S(2)}) %copy-start) | copy-done | bytes 1638424
  2.9 0.0 copy-start.2
  2.9 0.8 copy-done.2
  3.7 0.0 copy-start.3
  3.7 0.8 copy-done.3
  4.5 0.0 copy-start.5
  4.5 0.7 copy-done.5
  5.1 0.0 copy-start.1
  5.1 0.0 copy-start.4
  5.1 1.9 %shard_map.94.con_ref = f32[4,56,2048]{2,1,0:T(8,128)S(1)} custom-call(s32[4]{0:T(128)S(1)} %copy-done.5, f32[50,8192]{1,0:T(8,128)S(1)} %copy-done, f32[1,8192]{1,0:T(1,128)S(1)} %bitcast.6, s32[1,8192]{1,0:T(1,128)S(1)} %bitcast.7, f32[50,32]{1,0:T(8,128)S(1)} %copy.10.offsets_ref), custom_call_target="tpu_custom_call" | custom-call | tf_op jit(solution)/shard_map/pallas_call | solution.py:417
  7.0 0.0 copy-done.1
  7.0 0.0 copy-done.4
  7.0 84.6 %shard_map.95 = (f32[32,128]{1,0:T(8,128)S(1)}, f32[8,128]{1,0:T(8,128)S(1)}, f32[32,128]{1,0:T(8,128)S(1)}) custom-call(f32[4,56,2048]{2,1,0:T(8,128)S(1)} %shard_map.94.con_ref, f32[50,1024]{1,0:T(8,128)S(1)} %copy-done.1, f32[1,1024]{1,0:T(1,128)S(1)} %bitcast.10), custom_call_target="tpu_custom_call" | custom-call | tf_op jit(solution)/shard_map/pallas_call | solution.py:433
  91.6 0.6 copy.14
  92.2 0.6 copy.15
  92.8 0.6 copy.16
Async XLA Ops:
  1.4 1.5 %copy-start = (f32[50,8192]{1,0:T(8,128)S(1)}, f32[50,8192]{1,0:T(8,128)}, u32[]{:S(2)}) copy-start(f32[50,8192]{1,0:T(8,128)} %feats_ref.1) | copy-start | bytes 4915204
  2.9 0.8 copy-start.2
  3.7 0.8 copy-start.3
  4.5 0.7 copy-start.5
  5.1 1.9 %copy-start.1 = (f32[50,1024]{1,0:T(8,128)S(1)}, f32[50,1024]{1,0:T(8,128)}, u32[]{:S(2)}) copy-start(f32[50,1024]{1,0:T(8,128)} %tgt_ref.1) | copy-start | bytes 614404
  5.1 1.9 %copy-start.4 = (f32[1024]{0:T(1024)S(1)}, f32[1024]{0:T(1024)}, u32[]{:S(2)}) copy-start(f32[1024]{0:T(1024)} %param.13) | copy-start | bytes 12292

commit v2 on v1

--- a/solution.py
+++ b/solution.py
@@ -24,8 +24,8 @@
 F32 = jnp.float32
 BF16 = jnp.bfloat16
 MESH = pl.DeviceIdType.MESH
-TILE = 256
-CHUNK = 512
+TILE = 512
+CHUNK = 256
 
 
 def place():
@@ -52,46 +52,82 @@
     return high, middle, (rest - middle.astype(F32)).astype(BF16)
 
 
-def relay_kernel(counts_ref, feats_ref, mass_ref, ids_ref, offsets_ref, out_ref, held):
-    x_lo, core, z_hi, z_lo, y, x_hi = place()
-    mine = x_lo * 2 + core
-    start = jnp.int32(0)
-    for k in range(3):
-        start = start + jnp.where(k < mine, counts_ref[k], 0)
-    count = counts_ref[mine]
-    three = jnp.concatenate([p.astype(F32) for p in pieces(offsets_ref[...])], axis=1).astype(BF16)
+def correct(feats_ref, mass_ref, ids_ref, offsets_ref, held, ready):
+    three = jnp.concatenate([p.astype(F32) for p in pieces(offsets_ref[...])], axis=0).astype(BF16)
     for at in range(0, CAP, 1024):
+        ready(at)
         ids = ids_ref[:, at : at + 1024]
         section = lax.rem(lax.broadcasted_iota(jnp.int32, (3 * SECTIONS, 1024), 0), SECTIONS)
         onehot = jnp.where(section == ids, 1.0, 0.0).astype(BF16)
-        shift = jnp.dot(three, onehot, preferred_element_type=F32)
+        shift = lax.dot_general(
+            three, onehot, (((0,), (0,)), ((), ())), preferred_element_type=F32
+        )
         to = slice(LEAD + at, LEAD + at + 1024)
         held[48:ROWS, to] = jnp.zeros((ROWS - 48, 1024), F32)
         held[0:COMPONENTS, to] = feats_ref[:, at : at + 1024] - shift
         held[COMPONENTS : COMPONENTS + 1, to] = mass_ref[:, at : at + 1024]
+
+
+def contribute(held, base, count, out):
+    at = jnp.clip(base, -LEAD, CAP) + LEAD
+    aligned = pl.multiple_of(lax.div(at, 128) * 128, 128)
+    off = lax.rem(at, 128)
+    turn = lax.rem(128 - off, 128)
     lane = lax.broadcasted_iota(jnp.int32, (ROWS, 128), 1)
-
-    def contribute(index, carry):
-        to_x = lax.rem(x_lo + lax.div(index, 2), 2)
-        to_core = lax.rem(core + lax.rem(index, 2), 2)
-        base = (to_x * 2 + to_core) * (2 * GROUP) + z_lo * GROUP - start
-        at = jnp.clip(base, -LEAD, CAP) + LEAD
-        aligned = pl.multiple_of(lax.div(at, 128) * 128, 128)
-        off = lax.rem(at, 128)
-        turn = lax.rem(128 - off, 128)
-        before = pltpu.roll(held[:, pl.ds(aligned, 128)], turn, 1)
-        for t in range(GROUP // 128):
-            after = pltpu.roll(
-                held[:, pl.ds(pl.multiple_of(aligned + (t + 1) * 128, 128), 128)], turn, 1
-            )
-            value = jnp.where(lane < 128 - off, before, after)
-            local = lane + (base + t * 128)
-            value = jnp.where((local >= 0) & (local < count), value, 0.0)
-            out_ref[index, :, t * 128 : (t + 1) * 128] = value
-            before = after
-        return carry
-
-    lax.fori_loop(0, 4, contribute, 0)
+    before = pltpu.roll(held[:, pl.ds(aligned, 128)], turn, 1)
+    for t in range(GROUP // 128):
+        after = pltpu.roll(
+            held[:, pl.ds(pl.multiple_of(aligned + (t + 1) * 128, 128), 128)], turn, 1
+        )
+        value = jnp.where(lane < 128 - off, before, after)
+        local = lane + (base + t * 128)
+        out[:, t * 128 : (t + 1) * 128] = jnp.where((local >= 0) & (local < count), value, 0.0)
+        before = after
+
+
+def relay_kernel(
+    counts_ref, feats_any, mass_any, ids_any, offsets_any, out_any,
+    held, feats_ref, mass_ref, ids_ref, offsets_ref, out_ref, feats_sem, small_sem, out_sem,
+):
+    small = [
+        pltpu.make_async_copy(a, b, small_sem.at[i])
+        for i, (a, b) in enumerate(
+            [(offsets_any, offsets_ref), (ids_any, ids_ref), (mass_any, mass_ref)]
+        )
+    ]
+    large = [
+        pltpu.make_async_copy(
+            feats_any.at[:, at : at + 2048], feats_ref.at[:, at : at + 2048], feats_sem.at[i]
+        )
+        for i, at in enumerate(range(0, CAP, 2048))
+    ]
+    for copy in small + large:
+        copy.start()
+    x_lo, core, z_hi, z_lo, y, x_hi = place()
+    mine = x_lo * 2 + core
+    begin = jnp.int32(0)
+    for k in range(3):
+        begin = begin + jnp.where(k < mine, counts_ref[k], 0)
+    count = counts_ref[mine]
+
+    def ready(at):
+        if at % 2048 == 0:
+            large[at // 2048].wait()
+
+    for copy in small:
+        copy.wait()
+    correct(feats_ref, mass_ref, ids_ref, offsets_ref, held, ready)
+    moves = []
+    for index in (3, 2, 1, 0):
+        to_x, to_core = lax.rem(x_lo + index // 2, 2), lax.rem(core + index % 2, 2)
+        base = (to_x * 2 + to_core) * (2 * GROUP) + z_lo * GROUP - begin
+        contribute(held, base, count, out_ref.at[index])
+        moves.append(
+            pltpu.make_async_copy(out_ref.at[index], out_any.at[index], out_sem.at[index])
+        )
+        moves[-1].start()
+    for copy in moves:
+        copy.wait()
 
 
 def log_sum(parts):
@@ -170,16 +206,22 @@
 
 
 def sinkhorn_kernel(
-    con_ref, tgt_ref, mass_ref,
+    con_any, tgt_ref, tgt_mass_ref,
     src_out, tgt_out, self_out,
+    con_ref,
     from_own, from_opp, opp, landed, ybuf, xfull, sbuf,
     lhs_x, lhs_y, lhs_s, fix_x, fix_y, fix_s, rhs_x, rhs_y, buf_a, buf_b,
     sq_x, sq_y, sq_s, log_x, log_y, log_s, pot_p, pot_s, wide,
     fy, fz, py, pz, gb, pots, fin,
     relay_send, relay_recv, opp_send, opp_recv, own_sem, tgt_sem, self_sem, local_sem,
     fy_send, fy_recv, fz_send, fz_recv, py_send, py_recv, pz_send, pz_recv,
-    gb_send, gb_recv, pot_send, pot_recv, fin_send, fin_recv,
+    gb_send, gb_recv, pot_send, pot_recv, fin_send, fin_recv, con_sem,
 ):
+    loads = [
+        pltpu.make_async_copy(con_any.at[2 * i], con_ref.at[i], con_sem.at[i]) for i in range(2)
+    ]
+    for copy in loads:
+        copy.start()
     x_lo, core, z_hi, z_lo, y, x_hi = place()
     sibling = device(x_lo, 1 - core, z_hi, z_lo, y, x_hi)
     twin = device(x_lo, core, z_hi, 1 - z_lo, y, x_hi)
@@ -215,7 +257,7 @@
 
     ybuf[z_lo, 48:ROWS, :] = jnp.zeros((ROWS - 48, HALF), F32)
     ybuf[z_lo, 0:COMPONENTS, :] = tgt_ref[...]
-    ybuf[z_lo, COMPONENTS : COMPONENTS + 1, :] = mass_ref[...]
+    ybuf[z_lo, COMPONENTS : COMPONENTS + 1, :] = tgt_mass_ref[...]
 
     pl.semaphore_wait(barrier, len(peers))
 
@@ -227,22 +269,24 @@
 
     parts = [slice(c * 512, (c + 1) * 512) for c in range(4)]
     relays = [
-        remote(con_ref.at[3, :, s], from_opp.at[:, s], relay_send.at[c], relay_recv.at[c], sibling)
+        remote(con_any.at[3, :, s], from_opp.at[:, s], relay_send.at[c], relay_recv.at[c], sibling)
         for c, s in enumerate(parts)
     ]
+    own = remote(con_any.at[1], from_own, own_sem.at[0], own_sem.at[1], sibling)
+    tgt = remote(ybuf.at[z_lo], ybuf.at[z_lo], tgt_sem.at[0], tgt_sem.at[1], twin)
+    tgt.start()
+
     for copy in relays:
         copy.start()
-    own = remote(con_ref.at[1], from_own, own_sem.at[0], own_sem.at[1], sibling)
     own.start()
-    tgt = remote(ybuf.at[z_lo], ybuf.at[z_lo], tgt_sem.at[0], tgt_sem.at[1], twin)
-    tgt.start()
     onward = [
         remote(opp.at[:, s], landed.at[:, s], opp_send.at[c], opp_recv.at[c], opposite)
         for c, s in enumerate(parts)
     ]
+    loads[1].wait()
     for c, s in enumerate(parts):
         relays[c].wait_recv()
-        opp[:, s] = con_ref[2, :, s] + from_opp[:, s]
+        opp[:, s] = con_ref[1, :, s] + from_opp[:, s]
         onward[c].start()
 
     remote(ybuf.at[1 - z_lo], ybuf.at[1 - z_lo], tgt_sem.at[0], tgt_sem.at[1], twin).wait_recv()
@@ -256,6 +300,7 @@
     set_right(rhs_y, high, high, middle)
     set_weights(lhs_y, fix_y, log_y[...] - sq_y[...])
 
+    loads[0].wait()
     own.wait_recv()
     for copy in onward:
         copy.wait_recv()
@@ -286,8 +331,8 @@
     pot_s[...] = jnp.zeros_like(pot_s)
 
     def put_wide(j, value):
-        wide[pl.ds(2 * j, 1), :] = value[:, 0:128]
-        wide[pl.ds(2 * j + 1, 1), :] = value[:, 128:256]
+        for r in range(TILE // 128):
+            wide[pl.ds(TILE // 128 * j + r, 1), :] = value[:, r * 128 : (r + 1) * 128]
 
     def spread(box, it, me, others, peer, send, recv):
         for k in others:
@@ -414,21 +459,26 @@
     src_features, src_mass, section_ids, shard_counts, section_offsets, tgt_features, tgt_mass
 ):
     vmem = pl.BlockSpec(memory_space=pltpu.VMEM)
+    hbm = pl.BlockSpec(memory_space=pltpu.HBM)
+    V, D = pltpu.VMEM, pltpu.SemaphoreType.DMA
     contributions = pl.pallas_call(
         relay_kernel,
         out_shape=jax.ShapeDtypeStruct((4, ROWS, GROUP), F32),
-        in_specs=[pl.BlockSpec(memory_space=pltpu.SMEM)] + [vmem] * 4,
-        out_specs=vmem,
-        scratch_shapes=[pltpu.VMEM((ROWS, WIDTH), F32)],
-        compiler_params=pltpu.CompilerParams(vmem_limit_bytes=32 * 1024 * 1024),
+        in_specs=[pl.BlockSpec(memory_space=pltpu.SMEM)] + [hbm] * 4,
+        out_specs=hbm,
+        scratch_shapes=[
+            V((ROWS, WIDTH), F32), V((COMPONENTS, CAP), F32), V((1, CAP), F32),
+            V((1, CAP), jnp.int32), V((SECTIONS, COMPONENTS), F32), V((4, ROWS, GROUP), F32),
+            D((4,)), D((3,)), D((4,)),
+        ],
+        compiler_params=pltpu.CompilerParams(vmem_limit_bytes=58 * 1024 * 1024),
     )(
         shard_counts,
         src_features,
         src_mass.reshape(1, CAP),
         section_ids.reshape(1, CAP),
-        section_offsets,
+        section_offsets.T,
     )
-    V, D = pltpu.VMEM, pltpu.SemaphoreType.DMA
     rows16, rows8 = (16, 128), (8, 128)
     outs = pl.pallas_call(
         sinkhorn_kernel,
@@ -437,9 +487,10 @@
             jax.ShapeDtypeStruct((8, 128), F32),
             jax.ShapeDtypeStruct((32, 128), F32),
         ),
-        in_specs=[vmem] * 3,
+        in_specs=[hbm, vmem, vmem],
         out_specs=(vmem, vmem, vmem),
         scratch_shapes=[
+            V((2, ROWS, GROUP), F32),
             V((ROWS, GROUP), F32), V((ROWS, GROUP), F32), V((ROWS, GROUP), F32),
             V((ROWS, GROUP), F32), V((2, ROWS, HALF), F32), V((ROWS, GROUP), F32),
             V((ROWS, HALF), F32),
@@ -458,9 +509,10 @@
             D((ITERS, 4)), D((ITERS, 4)), D((ITERS, 4)), D((ITERS, 4)),
             D((ITERS, 4)), D((ITERS, 4)), D((ITERS, 4)), D((ITERS, 4)),
             D((ITERS, 8)), D((ITERS, 8)), D((ITERS,)), D((ITERS,)), D((2,)), D((2,)),
+            D((2,)),
         ],
         compiler_params=pltpu.CompilerParams(
-            collective_id=0, has_side_effects=True, vmem_limit_bytes=48 * 1024 * 1024
+            collective_id=0, has_side_effects=True, vmem_limit_bytes=58 * 1024 * 1024
         ),
     )(contributions, tgt_features, tgt_mass.reshape(1, HALF))
     return (outs[0].reshape(2 * GROUP), outs[1].reshape(HALF), outs[2].reshape(2 * GROUP))

time: 93.8 us -> 96 us (1.023)
  Pallas kernels: 86.5 us -> 91.1 us
  local copies, waits for them, and re-layouts: 6.29 us -> 3.91 us
    pallas_call x1, Pallas kernels: 1.87 us -> 4.37 us  [on_device(): pl.pallas_call(relay_kernel, out_shape=jax.ShapeDtypeStruct((4, ROWS, GRO...]
    unnamed x16 -> x3, local copies, waits for them, and re-layouts: 6.29 us -> 3.91 us
    pallas_call x1, Pallas kernels: 84.6 us -> 86.8 us  [on_device(): pl.pallas_call(sinkhorn_kernel, out_shape=(jax.ShapeDtypeStruct((32, 128)...]
where the time goes in v2:
time: 96 us; the launch traced here: 95.7 us
  Pallas kernels  91.1 us (95%)
  local copies, waits for them, and re-layouts  3.91 us (4%)
    pallas_call x1, Pallas kernels, on_device(): pl.pallas_call(sinkhorn_kernel, out_shape=(jax.ShapeDtypeStruct((32, 128)...  86.8 us
    pallas_call x1, Pallas kernels, on_device(): pl.pallas_call(relay_kernel, out_shape=jax.ShapeDtypeStruct((4, ROWS, GRO...  4.37 us
    unnamed x3, local copies, waits for them, and re-layouts  3.91 us

profile of v2, /device:TPU:1, one launch (start us, length us, event | category | flops | bytes accessed | tf_op | source)
XLA Modules:
  0.0 95.7 jit_solution(15681509413933153557)
XLA Ops:
  0.6 4.4 %shard_map.94.con_any = f32[4,56,2048]{2,1,0:T(8,128)} custom-call(s32[4]{0:T(128)} %counts_ref.1, f32[50,8192]{1,0:T(8,128)} %feats_any.1, f32[1,8192]{1,0:T(1,128)} %bitcast.7, s32[1,8192]{1,0:T(1,128)} %bitcast.8, f32[32,50]{1,0:T(8,128)} %bitcast.9), custom_call_target="tpu_custom_call" | custom-call | tf_op jit(solution)/shard_map/pallas_call | solution.py:464
  5.0 86.8 %shard_map.95 = (f32[32,128]{1,0:T(8,128)}, f32[8,128]{1,0:T(8,128)}, f32[32,128]{1,0:T(8,128)}) custom-call(f32[4,56,2048]{2,1,0:T(8,128)} %shard_map.94.con_any, f32[50,1024]{1,0:T(8,128)} %tgt_ref.1, f32[1,1024]{1,0:T(1,128)} %bitcast.12), custom_call_target="tpu_custom_call" | custom-call | tf_op jit(solution)/shard_map/pallas_call | solution.py:483
  91.8 1.3 %copy.13 = f32[4096]{0:T(1024)} copy(f32[4096]{0:T(1024)} %bitcast.11) | data formatting | bytes 32768
  93.1 1.3 %copy.14 = f32[1024]{0:T(1024)} copy(f32[1024]{0:T(1024)} %bitcast.13) | data formatting | bytes 8192
  94.4 1.3 %copy.15 = f32[4096]{0:T(1024)} copy(f32[4096]{0:T(1024)} %bitcast.10) | data formatting | bytes 32768

commit v3 on v2

--- a/solution.py
+++ b/solution.py
@@ -24,7 +24,8 @@
 F32 = jnp.float32
 BF16 = jnp.bfloat16
 MESH = pl.DeviceIdType.MESH
-TILE = 512
+TILE = 256
+TILES = GROUP // TILE
 CHUNK = 256
 
 
@@ -135,34 +136,92 @@
     return peak + jnp.log2(jnp.sum(jnp.exp2(parts - peak[None]), axis=0))
 
 
-def lse_pass(lhs, rhs, bufs, count, put):
-    tiles = GROUP // TILE
+def first_pass(lhs, rhs, cache, count, put):
     chunk = min(CHUNK, count)
 
-    def both(j_made, made, j_used, used, peak):
-        columns = rhs[:, pl.ds(pl.multiple_of(j_made * TILE, TILE), TILE)]
+    def both(j, peak):
         top, total = None, None
         for at in range(0, count, chunk):
-            s = jnp.dot(lhs[at : at + chunk, :], columns, preferred_element_type=F32)
-            made[at : at + chunk, :] = s
-            here = jnp.max(s, axis=0, keepdims=True)
-            top = here if top is None else jnp.maximum(top, here)
+            if j < TILES:
+                s = jnp.dot(
+                    lhs[at : at + chunk, :], rhs[:, j * TILE : (j + 1) * TILE],
+                    preferred_element_type=F32,
+                )
+                cache[j, at : at + chunk, :] = s
+                here = jnp.max(s, axis=0, keepdims=True)
+                top = here if top is None else jnp.maximum(top, here)
             if peak is not None:
-                e = jnp.exp2(used[at : at + chunk, :] - peak)
+                e = jnp.exp2(cache[j - 1, at : at + chunk, :] - peak)
                 part = jnp.sum(e, axis=0, keepdims=True)
                 total = part if total is None else total + part
         if peak is not None:
-            put(j_used, peak + jnp.log2(total))
+            put(j - 1, peak + jnp.log2(total))
         return top
 
-    first = both(0, bufs[0], None, None, None)
-
-    def body(pair, peak):
-        j = 2 * pair
-        peak = both(j + 1, bufs[1], j, bufs[0], peak)
-        return both(lax.rem(j + 2, tiles), bufs[0], j + 1, bufs[1], peak)
-
-    lax.fori_loop(0, tiles // 2, body, first)
+    peak = None
+    for j in range(TILES + 1):
+        peak = both(j, peak)
+
+
+def row_pass(cache, weight, count, put):
+    def body(j, carry):
+        peak, total = [None, None], [None, None]
+        for at in range(0, count, 128):
+            w = weight[at : at + 128, :]
+            for h in range(2):
+                t = (cache[j, at : at + 128, h * 128 : (h + 1) * 128] + w).reshape(16, 8, 128)
+                top = jnp.max(t, axis=0)
+                if at:
+                    top = jnp.maximum(top, peak[h])
+                part = jnp.sum(jnp.exp2(t - top[None]), axis=0)
+                if at:
+                    part = part + total[h] * jnp.exp2(peak[h] - top)
+                peak[h], total[h] = top, part
+        ends = []
+        for h in range(2):
+            top = jnp.max(peak[h], axis=0, keepdims=True)
+            part = jnp.sum(total[h] * jnp.exp2(peak[h] - top), axis=0, keepdims=True)
+            ends.append(top + jnp.log2(part))
+        put(j, jnp.concatenate(ends, axis=1))
+        return carry
+
+    lax.fori_loop(0, TILES, body, 0)
+
+
+def column_pass(cache, weight, spread_w, peaks, totals, out):
+    for r in range(16):
+        spread_w[r] = jnp.broadcast_to(weight[r : r + 1, :], (8, 128))
+
+    def body(block, carry):
+        for sub in range(4):
+            rows = pl.ds(pl.multiple_of(block * 64 + sub * 16, 16), 16)
+            parts = []
+            for r in range(16):
+                lanes = slice(r % 2 * 128, r % 2 * 128 + 128)
+                t = cache[r // 2, rows, lanes].reshape(2, 8, 128)
+                parts.append(t + spread_w[r][None])
+            tops = parts
+            while len(tops) > 1:
+                tops = [jnp.maximum(a, b) for a, b in zip(tops[0::2], tops[1::2])]
+            sums = [jnp.exp2(t - tops[0]) for t in parts]
+            while len(sums) > 1:
+                sums = [a + b for a, b in zip(sums[0::2], sums[1::2])]
+            peaks[rows, :] = tops[0].reshape(16, 128)
+            totals[rows, :] = sums[0].reshape(16, 128)
+        return carry
+
+    lax.fori_loop(0, GROUP // 64, body, 0)
+    for c in range(16):
+        at = slice(c * 128, (c + 1) * 128)
+        turned = peaks[at, :].T
+        top = jnp.max(turned, axis=0, keepdims=True)
+        total = jnp.sum(totals[at, :].T * jnp.exp2(turned - top), axis=0, keepdims=True)
+        out[c : c + 1, :] = top + jnp.log2(total)
+
+
+def spread_rows(wide_w, weight):
+    for c in range(weight.shape[0]):
+        wide_w[c * 128 : (c + 1) * 128, :] = jnp.broadcast_to(weight[c : c + 1, :], (128, 128)).T
 
 
 def to_rows(ref, row):
@@ -210,7 +269,8 @@
     src_out, tgt_out, self_out,
     con_ref,
     from_own, from_opp, opp, landed, ybuf, xfull, sbuf,
-    lhs_x, lhs_y, lhs_s, fix_x, fix_y, fix_s, rhs_x, rhs_y, buf_a, buf_b,
+    lhs_y, lhs_s, fix_y, fix_s, rhs_x, cache_f, cache_p,
+    spread_w, peaks, totals, wide_g, wide_s,
     sq_x, sq_y, sq_s, log_x, log_y, log_s, pot_p, pot_s, wide,
     fy, fz, py, pz, gb, pots, fin,
     relay_send, relay_recv, opp_send, opp_recv, own_sem, tgt_sem, self_sem, local_sem,
@@ -297,7 +357,6 @@
     to_rows(log_y, jnp.log2(cells[COMPONENTS : COMPONENTS + 1, :]))
     high, middle, unused = pieces(kept)
     set_left(lhs_y, fix_y, high, high, middle)
-    set_right(rhs_y, high, high, middle)
     set_weights(lhs_y, fix_y, log_y[...] - sq_y[...])
 
     loads[0].wait()
@@ -323,7 +382,6 @@
     to_rows(log_x, jnp.log2(cells[COMPONENTS : COMPONENTS + 1, :]))
     high, middle, unused = pieces(kept * (2.0 * SCALE))
     set_right(rhs_x, high, middle, high)
-    set_left(lhs_x, fix_x, high, middle, high)
     for copy in relays + onward + [own, tgt]:
         copy.wait_send()
 
@@ -345,11 +403,17 @@
             remote(box.at[it, me], box.at[it, me], send.at[it, k], recv.at[it, me], peer(k)).wait_send()
         return log_sum(box[it])
 
-    bufs = (buf_a, buf_b)
     half_rows = pl.ds(pl.multiple_of(x_hi * 8, 8), 8)
 
     def iteration(it, carry):
-        lse_pass(lhs_y, rhs_x, bufs, GROUP, put_wide)
+        @pl.when(it == 0)
+        def _():
+            first_pass(lhs_y, rhs_x, cache_f, GROUP, put_wide)
+
+        @pl.when(it > 0)
+        def _():
+            row_pass(cache_f, wide_g, GROUP, put_wide)
+
         fy[it, y] = wide[...] - sq_x[...]
         spread(fy, it, y, y_others, y_peer, fy_send, fy_recv)
 
@@ -370,6 +434,8 @@
             to_rows(log_s, jnp.log2(got[COMPONENTS : COMPONENTS + 1, :]))
             upper, lower, unused = pieces(columns)
             set_left(lhs_s, fix_s, upper, upper, lower)
+            set_weights(lhs_s, fix_s, log_s[...] - sq_s[...])
+            first_pass(lhs_s, rhs_x, cache_p, HALF, put_wide)
 
         @pl.when(it > 0)
         def _():
@@ -389,8 +455,9 @@
                 moved.wait_send()
                 pot_s[...] = pots[1, last]
 
-        set_weights(lhs_s, fix_s, log_s[...] + pot_s[...] - sq_s[...])
-        lse_pass(lhs_s, rhs_x, bufs, HALF, put_wide)
+            spread_rows(wide_s, pot_s[...])
+            row_pass(cache_p, wide_s, HALF, put_wide)
+
         py[it, y] = wide[...] - sq_x[...]
         spread(py, it, y, y_others, y_peer, py_send, py_recv)
 
@@ -399,8 +466,6 @@
         pz[it, zx] = collect(py, it, y, y_others, y_peer, py_send, py_recv)
         spread(pz, it, zx, zx_others, zx_peer, pz_send, pz_recv)
         pot_f = -TAU * collect(fz, it, zx, zx_others, zx_peer, fz_send, fz_recv)
-        set_weights(lhs_x, fix_x, log_x[...] + pot_f - sq_x[...])
-
         @pl.when(it == ITERS - 1)
         def _():
             fin[0, z_lo] = pot_f * (1.0 / SCALE)
@@ -408,8 +473,8 @@
                 fin.at[0, z_lo], fin.at[0, z_lo], fin_send.at[0], fin_recv.at[0], twin
             ).start()
 
-        lse_pass(lhs_x, rhs_y, bufs, GROUP, put_wide)
-        gb[it, g] = wide[...] - sq_y[...]
+        column_pass(cache_f, log_x[...] + pot_f - sq_x[...], spread_w, peaks, totals, wide)
+        gb[it, g] = wide[...] - log_y[...]
         spread(gb, it, g, g_others, g_peer, gb_send, gb_recv)
 
         new_p = -TAU * collect(pz, it, zx, zx_others, zx_peer, pz_send, pz_recv)
@@ -434,7 +499,7 @@
 
         @pl.when(it < ITERS - 1)
         def _():
-            set_weights(lhs_y, fix_y, log_y[...] + pot_g - sq_y[...])
+            spread_rows(wide_g, pot_g)
 
         return carry
 
@@ -483,9 +548,7 @@
     outs = pl.pallas_call(
         sinkhorn_kernel,
         out_shape=(
-            jax.ShapeDtypeStruct((32, 128), F32),
-            jax.ShapeDtypeStruct((8, 128), F32),
-            jax.ShapeDtypeStruct((32, 128), F32),
+            V((32, 128), F32), V((8, 128), F32), V((32, 128), F32),
         ),
         in_specs=[hbm, vmem, vmem],
         out_specs=(vmem, vmem, vmem),
@@ -494,10 +557,11 @@
             V((ROWS, GROUP), F32), V((ROWS, GROUP), F32), V((ROWS, GROUP), F32),
             V((ROWS, GROUP), F32), V((2, ROWS, HALF), F32), V((ROWS, GROUP), F32),
             V((ROWS, HALF), F32),
-            V((GROUP, 256), BF16), V((GROUP, 256), BF16), V((HALF, 256), BF16),
-            V((GROUP, 128), BF16), V((GROUP, 128), BF16), V((HALF, 128), BF16),
-            V((256, GROUP), BF16), V((256, GROUP), BF16),
-            V((GROUP, TILE), F32), V((GROUP, TILE), F32),
+            V((GROUP, 256), BF16), V((HALF, 256), BF16),
+            V((GROUP, 128), BF16), V((HALF, 128), BF16), V((256, GROUP), BF16),
+            V((TILES, GROUP, TILE), F32), V((TILES, HALF, TILE), F32),
+            V((16, 8, 128), F32), V((GROUP, 128), F32), V((GROUP, 128), F32),
+            V((GROUP, 128), F32), V((HALF, 128), F32),
             V(rows16, F32), V(rows16, F32), V(rows8, F32),
             V(rows16, F32), V(rows16, F32), V(rows8, F32),
             V(rows16, F32), V(rows8, F32), V(rows16, F32),

time: 96 us -> 84.8 us (0.88)
  Pallas kernels: 91.1 us -> 82.2 us
  local copies, waits for them, and re-layouts: 3.91 us -> 1.81 us
    pallas_call x1, Pallas kernels: 86.8 us -> 77.8 us  [on_device(): pl.pallas_call(sinkhorn_kernel, out_shape=(V((32, 128), F32), V((8, 128),...]
    unnamed x3, local copies, waits for them, and re-layouts: 3.91 us -> 1.81 us
where the time goes in v3:
time: 84.8 us; the launch traced here: 84.6 us
  Pallas kernels  82.2 us (97%)
  local copies, waits for them, and re-layouts  1.81 us (2%)
    pallas_call x1, Pallas kernels, on_device(): pl.pallas_call(sinkhorn_kernel, out_shape=(V((32, 128), F32), V((8, 128),...  77.8 us
    pallas_call x1, Pallas kernels, on_device(): pl.pallas_call(relay_kernel, out_shape=jax.ShapeDtypeStruct((4, ROWS, GRO...  4.37 us
    unnamed x3, local copies, waits for them, and re-layouts  1.81 us

profile of v3, /device:TPU:1, one launch (start us, length us, event | category | flops | bytes accessed | tf_op | source)
XLA Modules:
  0.0 84.6 jit_solution(1776092619168597487)
XLA Ops:
  0.6 4.4 %shard_map.94.con_any = f32[4,56,2048]{2,1,0:T(8,128)} custom-call(s32[4]{0:T(128)} %counts_ref.1, f32[50,8192]{1,0:T(8,128)} %feats_any.1, f32[1,8192]{1,0:T(1,128)} %bitcast.10, s32[1,8192]{1,0:T(1,128)} %bitcast.11, f32[32,50]{1,0:T(8,128)} %bitcast.12), custom_call_target="tpu_custom_call" | custom-call | tf_op jit(solution)/shard_map/pallas_call | solution.py:529
  5.0 77.8 %shard_map.95 = (f32[32,128]{1,0:T(8,128)S(1)}, f32[8,128]{1,0:T(8,128)S(1)}, f32[32,128]{1,0:T(8,128)S(1)}) custom-call(f32[4,56,2048]{2,1,0:T(8,128)} %shard_map.94.con_any, f32[50,1024]{1,0:T(8,128)} %tgt_ref.1, f32[1,1024]{1,0:T(1,128)} %bitcast.13), custom_call_target="tpu_custom_call" | custom-call | tf_op jit(solution)/shard_map/pallas_call | solution.py:548
  82.8 0.6 copy.13
  83.4 0.6 copy.14
  84.0 0.6 copy.15

commit v4 on v3

--- a/solution.py
+++ b/solution.py
@@ -272,9 +272,9 @@
     lhs_y, lhs_s, fix_y, fix_s, rhs_x, cache_f, cache_p,
     spread_w, peaks, totals, wide_g, wide_s,
     sq_x, sq_y, sq_s, log_x, log_y, log_s, pot_p, pot_s, wide,
-    fy, fz, py, pz, gb, pots, fin,
+    fb, pb, gb, pots, fin,
     relay_send, relay_recv, opp_send, opp_recv, own_sem, tgt_sem, self_sem, local_sem,
-    fy_send, fy_recv, fz_send, fz_recv, py_send, py_recv, pz_send, pz_recv,
+    fb_send, fb_recv, pb_send, pb_recv,
     gb_send, gb_recv, pot_send, pot_recv, fin_send, fin_recv, con_sem,
 ):
     loads = [
@@ -294,23 +294,19 @@
     )
     alone = (y + z_hi) == 0
     g = x_lo * 4 + core * 2 + z_lo
-    zx = z_hi * 2 + x_hi
-
-    def y_peer(k):
-        return device(x_lo, core, z_hi, z_lo, k, x_hi)
-
-    def zx_peer(k):
-        return device(x_lo, core, lax.div(k, 2), z_lo, y, lax.rem(k, 2))
+    m = z_hi * 8 + y * 2 + x_hi
+
+    def m_peer(k):
+        return device(x_lo, core, lax.div(k, 8), z_lo, lax.rem(lax.div(k, 2), 4), lax.rem(k, 2))
 
     def g_peer(k):
         return device(lax.div(k, 4), lax.rem(lax.div(k, 2), 2), z_hi, lax.rem(k, 2), y, x_hi)
 
-    y_others = [lax.rem(y + d, 4) for d in range(1, 4)]
-    zx_others = [lax.rem(zx + d, 4) for d in range(1, 4)]
+    m_others = [lax.rem(m + d, 16) for d in range(1, 16)]
     g_others = [lax.rem(g + d, 8) for d in range(1, 8)]
 
     barrier = pltpu.get_barrier_semaphore()
-    peers = [y_peer(k) for k in y_others] + [zx_peer(k) for k in zx_others]
+    peers = [m_peer(k) for k in m_others]
     peers += [g_peer(k) for k in g_others] + [across]
     for peer in peers:
         pl.semaphore_signal(barrier, inc=1, device_id=peer, device_id_type=MESH)
@@ -414,8 +410,8 @@
         def _():
             row_pass(cache_f, wide_g, GROUP, put_wide)
 
-        fy[it, y] = wide[...] - sq_x[...]
-        spread(fy, it, y, y_others, y_peer, fy_send, fy_recv)
+        fb[it, m] = wide[...] - sq_x[...]
+        spread(fb, it, m, m_others, m_peer, fb_send, fb_recv)
 
         @pl.when(it == 0)
         def _():
@@ -458,14 +454,10 @@
             spread_rows(wide_s, pot_s[...])
             row_pass(cache_p, wide_s, HALF, put_wide)
 
-        py[it, y] = wide[...] - sq_x[...]
-        spread(py, it, y, y_others, y_peer, py_send, py_recv)
-
-        fz[it, zx] = collect(fy, it, y, y_others, y_peer, fy_send, fy_recv)
-        spread(fz, it, zx, zx_others, zx_peer, fz_send, fz_recv)
-        pz[it, zx] = collect(py, it, y, y_others, y_peer, py_send, py_recv)
-        spread(pz, it, zx, zx_others, zx_peer, pz_send, pz_recv)
-        pot_f = -TAU * collect(fz, it, zx, zx_others, zx_peer, fz_send, fz_recv)
+        pb[it, m] = wide[...] - sq_x[...]
+        spread(pb, it, m, m_others, m_peer, pb_send, pb_recv)
+
+        pot_f = -TAU * collect(fb, it, m, m_others, m_peer, fb_send, fb_recv)
         @pl.when(it == ITERS - 1)
         def _():
             fin[0, z_lo] = pot_f * (1.0 / SCALE)
@@ -477,7 +469,7 @@
         gb[it, g] = wide[...] - log_y[...]
         spread(gb, it, g, g_others, g_peer, gb_send, gb_recv)
 
-        new_p = -TAU * collect(pz, it, zx, zx_others, zx_peer, pz_send, pz_recv)
+        new_p = -TAU * collect(pb, it, m, m_others, m_peer, pb_send, pb_recv)
         pot_p[...] = 0.5 * (pot_p[...] + new_p)
 
         @pl.when((it < ITERS - 1) & jnp.logical_not(alone))
@@ -565,13 +557,11 @@
             V(rows16, F32), V(rows16, F32), V(rows8, F32),
             V(rows16, F32), V(rows16, F32), V(rows8, F32),
             V(rows16, F32), V(rows8, F32), V(rows16, F32),
-            V((ITERS, 4) + rows16, F32), V((ITERS, 4) + rows16, F32),
-            V((ITERS, 4) + rows16, F32), V((ITERS, 4) + rows16, F32),
+            V((ITERS, 16) + rows16, F32), V((ITERS, 16) + rows16, F32),
             V((ITERS, 8) + rows16, F32), V((2, ITERS - 1) + rows8, F32),
             V((2, 2) + rows16, F32),
             D((4,)), D((4,)), D((4,)), D((4,)), D((2,)), D((2,)), D((2,)), D,
-            D((ITERS, 4)), D((ITERS, 4)), D((ITERS, 4)), D((ITERS, 4)),
-            D((ITERS, 4)), D((ITERS, 4)), D((ITERS, 4)), D((ITERS, 4)),
+            D((ITERS, 16)), D((ITERS, 16)), D((ITERS, 16)), D((ITERS, 16)),
             D((ITERS, 8)), D((ITERS, 8)), D((ITERS,)), D((ITERS,)), D((2,)), D((2,)),
             D((2,)),
         ],

time: 84.8 us -> 79.5 us (0.938)
  Pallas kernels: 82.2 us -> 76.9 us
    pallas_call x1, Pallas kernels: 77.8 us -> 72.5 us  [on_device(): pl.pallas_call(sinkhorn_kernel, out_shape=(V((32, 128), F32), V((8, 128),...]
where the time goes in v4:
time: 79.5 us; the launch traced here: 79.4 us
  Pallas kernels  76.9 us (97%)
  local copies, waits for them, and re-layouts  1.81 us (2%)
    pallas_call x1, Pallas kernels, on_device(): pl.pallas_call(sinkhorn_kernel, out_shape=(V((32, 128), F32), V((8, 128),...  72.5 us
    pallas_call x1, Pallas kernels, on_device(): pl.pallas_call(relay_kernel, out_shape=jax.ShapeDtypeStruct((4, ROWS, GRO...  4.37 us
    unnamed x3, local copies, waits for them, and re-layouts  1.81 us

profile of v4, /device:TPU:1, one launch (start us, length us, event | category | flops | bytes accessed | tf_op | source)
XLA Modules:
  0.0 79.4 jit_solution(13644377786204140806)
XLA Ops:
  0.6 4.4 %shard_map.94.con_any = f32[4,56,2048]{2,1,0:T(8,128)} custom-call(s32[4]{0:T(128)} %counts_ref.1, f32[50,8192]{1,0:T(8,128)} %feats_any.1, f32[1,8192]{1,0:T(1,128)} %bitcast.10, s32[1,8192]{1,0:T(1,128)} %bitcast.11, f32[32,50]{1,0:T(8,128)} %bitcast.12), custom_call_target="tpu_custom_call" | custom-call | tf_op jit(solution)/shard_map/pallas_call | solution.py:521
  5.0 72.5 %shard_map.95 = (f32[32,128]{1,0:T(8,128)S(1)}, f32[8,128]{1,0:T(8,128)S(1)}, f32[32,128]{1,0:T(8,128)S(1)}) custom-call(f32[4,56,2048]{2,1,0:T(8,128)} %shard_map.94.con_any, f32[50,1024]{1,0:T(8,128)} %tgt_ref.1, f32[1,1024]{1,0:T(1,128)} %bitcast.13), custom_call_target="tpu_custom_call" | custom-call | tf_op jit(solution)/shard_map/pallas_call | solution.py:540
  77.5 0.6 copy.13
  78.2 0.6 copy.14
  78.7 0.6 copy.15

commit v5 on v4

--- a/solution.py
+++ b/solution.py
@@ -136,7 +136,7 @@
     return peak + jnp.log2(jnp.sum(jnp.exp2(parts - peak[None]), axis=0))
 
 
-def first_pass(lhs, rhs, cache, count, put):
+def first_pass(lhs, rhs, cache, count, put, ready=None):
     chunk = min(CHUNK, count)
 
     def both(j, peak):
@@ -160,6 +160,8 @@
 
     peak = None
     for j in range(TILES + 1):
+        if ready is not None and j < TILES:
+            ready(j)
         peak = both(j, peak)
 
 
@@ -224,9 +226,9 @@
         wide_w[c * 128 : (c + 1) * 128, :] = jnp.broadcast_to(weight[c : c + 1, :], (128, 128)).T
 
 
-def to_rows(ref, row):
+def to_rows(ref, row, first=0):
     for r in range(row.shape[1] // 128):
-        ref[r : r + 1, :] = row[:, r * 128 : (r + 1) * 128]
+        ref[first + r : first + r + 1, :] = row[:, r * 128 : (r + 1) * 128]
 
 
 def set_weights(lhs, fixed, weight):
@@ -250,12 +252,12 @@
         fixed[at, :] = second.T.astype(BF16)
 
 
-def set_right(rhs, one, two, three):
-    rhs[0:64, :] = one
-    rhs[64:128, :] = two
-    row = lax.broadcasted_iota(jnp.int32, (64, GROUP), 0)
-    rhs[128:192, :] = jnp.where(row < 48, 1.0, 0.0).astype(BF16)
-    rhs[192:256, :] = three
+def set_right(rhs, at, one, two, three):
+    rhs[0:64, at] = one
+    rhs[64:128, at] = two
+    row = lax.broadcasted_iota(jnp.int32, three.shape, 0)
+    rhs[128:192, at] = jnp.where(row < 48, 1.0, 0.0).astype(BF16)
+    rhs[192:256, at] = three
 
 
 def padded(cells, centre):
@@ -265,9 +267,9 @@
 
 
 def sinkhorn_kernel(
-    con_any, tgt_ref, tgt_mass_ref,
+    con_any, tgt_any, tgt_mass_any,
     src_out, tgt_out, self_out,
-    con_ref,
+    con_ref, tgt_ref, tgt_mass_ref,
     from_own, from_opp, opp, landed, ybuf, xfull, sbuf,
     lhs_y, lhs_s, fix_y, fix_s, rhs_x, cache_f, cache_p,
     spread_w, peaks, totals, wide_g, wide_s,
@@ -277,11 +279,6 @@
     fb_send, fb_recv, pb_send, pb_recv,
     gb_send, gb_recv, pot_send, pot_recv, fin_send, fin_recv, con_sem,
 ):
-    loads = [
-        pltpu.make_async_copy(con_any.at[2 * i], con_ref.at[i], con_sem.at[i]) for i in range(2)
-    ]
-    for copy in loads:
-        copy.start()
     x_lo, core, z_hi, z_lo, y, x_hi = place()
     sibling = device(x_lo, 1 - core, z_hi, z_lo, y, x_hi)
     twin = device(x_lo, core, z_hi, 1 - z_lo, y, x_hi)
@@ -311,6 +308,21 @@
     for peer in peers:
         pl.semaphore_signal(barrier, inc=1, device_id=peer, device_id_type=MESH)
 
+    loads = [
+        pltpu.make_async_copy(a, b, con_sem.at[i])
+        for i, (a, b) in enumerate(
+            [
+                (tgt_any, tgt_ref),
+                (tgt_mass_any, tgt_mass_ref),
+                (con_any.at[2], con_ref.at[1]),
+                (con_any.at[0], con_ref.at[0]),
+            ]
+        )
+    ]
+    for copy in loads:
+        copy.start()
+    loads[0].wait()
+    loads[1].wait()
     ybuf[z_lo, 48:ROWS, :] = jnp.zeros((ROWS - 48, HALF), F32)
     ybuf[z_lo, 0:COMPONENTS, :] = tgt_ref[...]
     ybuf[z_lo, COMPONENTS : COMPONENTS + 1, :] = tgt_mass_ref[...]
@@ -339,7 +351,7 @@
         remote(opp.at[:, s], landed.at[:, s], opp_send.at[c], opp_recv.at[c], opposite)
         for c, s in enumerate(parts)
     ]
-    loads[1].wait()
+    loads[2].wait()
     for c, s in enumerate(parts):
         relays[c].wait_recv()
         opp[:, s] = con_ref[1, :, s] + from_opp[:, s]
@@ -355,12 +367,28 @@
     set_left(lhs_y, fix_y, high, high, middle)
     set_weights(lhs_y, fix_y, log_y[...] - sq_y[...])
 
-    loads[0].wait()
+    def put_wide(j, value):
+        for r in range(TILE // 128):
+            wide[pl.ds(TILE // 128 * j + r, 1), :] = value[:, r * 128 : (r + 1) * 128]
+
+    loads[3].wait()
     own.wait_recv()
-    for copy in onward:
-        copy.wait_recv()
-    cells = con_ref[0] + from_own[...] + landed[...]
-    xfull[...] = cells
+
+    def arrive(j):
+        if j % 2:
+            return
+        c = j // 2
+        s = parts[c]
+        onward[c].wait_recv()
+        cells = con_ref[0, :, s] + from_own[:, s] + landed[:, s]
+        xfull[:, s] = cells
+        kept = padded(cells, centre)
+        to_rows(sq_x, jnp.sum(kept * kept, axis=0, keepdims=True) * SCALE, 4 * c)
+        to_rows(log_x, jnp.log2(cells[COMPONENTS : COMPONENTS + 1, :]), 4 * c)
+        high, middle, unused = pieces(kept * (2.0 * SCALE))
+        set_right(rhs_x, s, high, middle, high)
+
+    first_pass(lhs_y, rhs_x, cache_f, GROUP, put_wide, arrive)
     half = pl.ds(pl.multiple_of(x_hi * HALF, HALF), HALF)
     shared = remote(xfull.at[:, half], sbuf, self_sem.at[0], self_sem.at[1], partner)
     kept_here = pltpu.make_async_copy(xfull.at[:, half], sbuf, local_sem)
@@ -373,45 +401,28 @@
     def _():
         shared.start()
 
-    kept = padded(cells, centre)
-    to_rows(sq_x, jnp.sum(kept * kept, axis=0, keepdims=True) * SCALE)
-    to_rows(log_x, jnp.log2(cells[COMPONENTS : COMPONENTS + 1, :]))
-    high, middle, unused = pieces(kept * (2.0 * SCALE))
-    set_right(rhs_x, high, middle, high)
-    for copy in relays + onward + [own, tgt]:
-        copy.wait_send()
-
     pot_p[...] = jnp.zeros_like(pot_p)
     pot_s[...] = jnp.zeros_like(pot_s)
 
-    def put_wide(j, value):
-        for r in range(TILE // 128):
-            wide[pl.ds(TILE // 128 * j + r, 1), :] = value[:, r * 128 : (r + 1) * 128]
-
     def spread(box, it, me, others, peer, send, recv):
         for k in others:
-            remote(box.at[it, me], box.at[it, me], send.at[it, k], recv.at[it, me], peer(k)).start()
-
-    def collect(box, it, me, others, peer, send, recv):
-        for k in others:
-            remote(box.at[it, k], box.at[it, k], send.at[it, k], recv.at[it, k], peer(k)).wait_recv()
-        for k in others:
-            remote(box.at[it, me], box.at[it, me], send.at[it, k], recv.at[it, me], peer(k)).wait_send()
-        return log_sum(box[it])
+            remote(box.at[it, me], box.at[it, me], send.at[it], recv.at[it], peer(k)).start()
+
+    def all_of(box, it, others, peer, send, recv):
+        part = box.at[it, pl.ds(0, len(others))]
+        return remote(part, part, send.at[it], recv.at[it], peer(others[0]))
+
+    to_m, to_g = (m_others, m_peer), (g_others, g_peer)
 
     half_rows = pl.ds(pl.multiple_of(x_hi * 8, 8), 8)
 
     def iteration(it, carry):
-        @pl.when(it == 0)
-        def _():
-            first_pass(lhs_y, rhs_x, cache_f, GROUP, put_wide)
-
         @pl.when(it > 0)
         def _():
             row_pass(cache_f, wide_g, GROUP, put_wide)
 
         fb[it, m] = wide[...] - sq_x[...]
-        spread(fb, it, m, m_others, m_peer, fb_send, fb_recv)
+        spread(fb, it, m, *to_m, fb_send, fb_recv)
 
         @pl.when(it == 0)
         def _():
@@ -424,6 +435,8 @@
                 shared.wait_recv()
                 shared.wait_send()
 
+            for copy in relays + onward + [own, tgt]:
+                copy.wait_send()
             got = sbuf[...]
             columns = padded(got, centre)
             to_rows(sq_s, jnp.sum(columns * columns, axis=0, keepdims=True) * SCALE)
@@ -455,9 +468,10 @@
             row_pass(cache_p, wide_s, HALF, put_wide)
 
         pb[it, m] = wide[...] - sq_x[...]
-        spread(pb, it, m, m_others, m_peer, pb_send, pb_recv)
-
-        pot_f = -TAU * collect(fb, it, m, m_others, m_peer, fb_send, fb_recv)
+        spread(pb, it, m, *to_m, pb_send, pb_recv)
+
+        all_of(fb, it, *to_m, fb_send, fb_recv).wait_recv()
+        pot_f = -TAU * log_sum(fb[it])
         @pl.when(it == ITERS - 1)
         def _():
             fin[0, z_lo] = pot_f * (1.0 / SCALE)
@@ -467,9 +481,10 @@
 
         column_pass(cache_f, log_x[...] + pot_f - sq_x[...], spread_w, peaks, totals, wide)
         gb[it, g] = wide[...] - log_y[...]
-        spread(gb, it, g, g_others, g_peer, gb_send, gb_recv)
-
-        new_p = -TAU * collect(pb, it, m, m_others, m_peer, pb_send, pb_recv)
+        spread(gb, it, g, *to_g, gb_send, gb_recv)
+
+        all_of(pb, it, *to_m, pb_send, pb_recv).wait_recv()
+        new_p = -TAU * log_sum(pb[it])
         pot_p[...] = 0.5 * (pot_p[...] + new_p)
 
         @pl.when((it < ITERS - 1) & jnp.logical_not(alone))
@@ -486,7 +501,11 @@
                 fin.at[1, z_lo], fin.at[1, z_lo], fin_send.at[1], fin_recv.at[1], twin
             ).start()
 
-        pot_g = -TAU * collect(gb, it, g, g_others, g_peer, gb_send, gb_recv)
+        all_of(fb, it, *to_m, fb_send, fb_recv).wait_send()
+        all_of(pb, it, *to_m, pb_send, pb_recv).wait_send()
+        all_of(gb, it, *to_g, gb_send, gb_recv).wait_send()
+        all_of(gb, it, *to_g, gb_send, gb_recv).wait_recv()
+        pot_g = -TAU * log_sum(gb[it])
         wide[...] = pot_g
 
         @pl.when(it < ITERS - 1)
@@ -542,10 +561,10 @@
         out_shape=(
             V((32, 128), F32), V((8, 128), F32), V((32, 128), F32),
         ),
-        in_specs=[hbm, vmem, vmem],
+        in_specs=[hbm] * 3,
         out_specs=(vmem, vmem, vmem),
         scratch_shapes=[
-            V((2, ROWS, GROUP), F32),
+            V((2, ROWS, GROUP), F32), V((COMPONENTS, HALF), F32), V((1, HALF), F32),
             V((ROWS, GROUP), F32), V((ROWS, GROUP), F32), V((ROWS, GROUP), F32),
             V((ROWS, GROUP), F32), V((2, ROWS, HALF), F32), V((ROWS, GROUP), F32),
             V((ROWS, HALF), F32),
@@ -561,9 +580,9 @@
             V((ITERS, 8) + rows16, F32), V((2, ITERS - 1) + rows8, F32),
             V((2, 2) + rows16, F32),
             D((4,)), D((4,)), D((4,)), D((4,)), D((2,)), D((2,)), D((2,)), D,
-            D((ITERS, 16)), D((ITERS, 16)), D((ITERS, 16)), D((ITERS, 16)),
-            D((ITERS, 8)), D((ITERS, 8)), D((ITERS,)), D((ITERS,)), D((2,)), D((2,)),
-            D((2,)),
+            D((ITERS,)), D((ITERS,)), D((ITERS,)), D((ITERS,)), D((ITERS,)), D((ITERS,)),
+            D((ITERS,)), D((ITERS,)), D((2,)), D((2,)),
+            D((4,)),
         ],
         compiler_params=pltpu.CompilerParams(
             collective_id=0, has_side_effects=True, vmem_limit_bytes=58 * 1024 * 1024

time: 79.5 us -> 81.5 us (1.025)
  Pallas kernels: 76.9 us -> 78.8 us
    pallas_call x1, Pallas kernels: 72.5 us -> 74.5 us  [on_device(): pl.pallas_call(sinkhorn_kernel, out_shape=(V((32, 128), F32), V((8, 128),...]
where the time goes in v5:
time: 81.5 us; the launch traced here: 81.3 us
  Pallas kernels  78.8 us (97%)
  local copies, waits for them, and re-layouts  1.81 us (2%)
    pallas_call x1, Pallas kernels, on_device(): pl.pallas_call(sinkhorn_kernel, out_shape=(V((32, 128), F32), V((8, 128),...  74.5 us
    pallas_call x1, Pallas kernels, on_device(): pl.pallas_call(relay_kernel, out_shape=jax.ShapeDtypeStruct((4, ROWS, GRO...  4.37 us
    unnamed x3, local copies, waits for them, and re-layouts  1.81 us

profile of v5, /device:TPU:1, one launch (start us, length us, event | category | flops | bytes accessed | tf_op | source)
XLA Modules:
  0.0 81.3 jit_solution(560537804742009381)
XLA Ops:
  0.6 4.4 %shard_map.94.con_any = f32[4,56,2048]{2,1,0:T(8,128)} custom-call(s32[4]{0:T(128)} %counts_ref.1, f32[50,8192]{1,0:T(8,128)} %feats_any.1, f32[1,8192]{1,0:T(1,128)} %bitcast.10, s32[1,8192]{1,0:T(1,128)} %bitcast.11, f32[32,50]{1,0:T(8,128)} %bitcast.12), custom_call_target="tpu_custom_call" | custom-call | tf_op jit(solution)/shard_map/pallas_call | solution.py:540
  5.0 74.5 %shard_map.95 = (f32[32,128]{1,0:T(8,128)S(1)}, f32[8,128]{1,0:T(8,128)S(1)}, f32[32,128]{1,0:T(8,128)S(1)}) custom-call(f32[4,56,2048]{2,1,0:T(8,128)} %shard_map.94.con_any, f32[50,1024]{1,0:T(8,128)} %tgt_any.1, f32[1,1024]{1,0:T(1,128)} %bitcast.13), custom_call_target="tpu_custom_call" | custom-call | tf_op jit(solution)/shard_map/pallas_call | solution.py:559
  79.5 0.6 copy.13
  80.1 0.6 copy.14
  80.7 0.6 copy.15

commit v6 on v5

--- a/solution.py
+++ b/solution.py
@@ -195,8 +195,8 @@
         spread_w[r] = jnp.broadcast_to(weight[r : r + 1, :], (8, 128))
 
     def body(block, carry):
-        for sub in range(4):
-            rows = pl.ds(pl.multiple_of(block * 64 + sub * 16, 16), 16)
+        for sub in range(8):
+            rows = pl.ds(pl.multiple_of(block * 128 + sub * 16, 16), 16)
             parts = []
             for r in range(16):
                 lanes = slice(r % 2 * 128, r % 2 * 128 + 128)
@@ -212,7 +212,7 @@
             totals[rows, :] = sums[0].reshape(16, 128)
         return carry
 
-    lax.fori_loop(0, GROUP // 64, body, 0)
+    lax.fori_loop(0, GROUP // 128, body, 0)
     for c in range(16):
         at = slice(c * 128, (c + 1) * 128)
         turned = peaks[at, :].T
@@ -374,6 +374,10 @@
     loads[3].wait()
     own.wait_recv()
 
+    half = pl.ds(pl.multiple_of(x_hi * HALF, HALF), HALF)
+    shared = remote(xfull.at[:, half], sbuf, self_sem.at[0], self_sem.at[1], partner)
+    kept_here = pltpu.make_async_copy(xfull.at[:, half], sbuf, local_sem)
+
     def arrive(j):
         if j % 2:
             return
@@ -382,6 +386,15 @@
         onward[c].wait_recv()
         cells = con_ref[0, :, s] + from_own[:, s] + landed[:, s]
         xfull[:, s] = cells
+        if c % 2:
+            @pl.when((x_hi == c // 2) & alone)
+            def _():
+                kept_here.start()
+
+            @pl.when((x_hi == c // 2) & jnp.logical_not(alone))
+            def _():
+                shared.start()
+
         kept = padded(cells, centre)
         to_rows(sq_x, jnp.sum(kept * kept, axis=0, keepdims=True) * SCALE, 4 * c)
         to_rows(log_x, jnp.log2(cells[COMPONENTS : COMPONENTS + 1, :]), 4 * c)
@@ -389,17 +402,6 @@
         set_right(rhs_x, s, high, middle, high)
 
     first_pass(lhs_y, rhs_x, cache_f, GROUP, put_wide, arrive)
-    half = pl.ds(pl.multiple_of(x_hi * HALF, HALF), HALF)
-    shared = remote(xfull.at[:, half], sbuf, self_sem.at[0], self_sem.at[1], partner)
-    kept_here = pltpu.make_async_copy(xfull.at[:, half], sbuf, local_sem)
-
-    @pl.when(alone)
-    def _():
-        kept_here.start()
-
-    @pl.when(jnp.logical_not(alone))
-    def _():
-        shared.start()
 
     pot_p[...] = jnp.zeros_like(pot_p)
     pot_s[...] = jnp.zeros_like(pot_s)
@@ -415,6 +417,18 @@
     to_m, to_g = (m_others, m_peer), (g_others, g_peer)
 
     half_rows = pl.ds(pl.multiple_of(x_hi * 8, 8), 8)
+
+    def finish_p(it):
+        all_of(pb, it, *to_m, pb_send, pb_recv).wait_recv()
+        all_of(pb, it, *to_m, pb_send, pb_recv).wait_send()
+        pot_p[...] = 0.5 * (pot_p[...] - TAU * log_sum(pb[it]))
+
+        @pl.when((it < ITERS - 1) & jnp.logical_not(alone))
+        def _():
+            pots[0, it] = pot_p[half_rows, :]
+            remote(
+                pots.at[0, it], pots.at[1, it], pot_send.at[it], pot_recv.at[it], partner
+            ).start()
 
     def iteration(it, carry):
         @pl.when(it > 0)
@@ -444,7 +458,10 @@
             upper, lower, unused = pieces(columns)
             set_left(lhs_s, fix_s, upper, upper, lower)
             set_weights(lhs_s, fix_s, log_s[...] - sq_s[...])
-            first_pass(lhs_s, rhs_x, cache_p, HALF, put_wide)
+
+        @pl.when(it == 1)
+        def _():
+            finish_p(0)
 
         @pl.when(it > 0)
         def _():
@@ -466,9 +483,8 @@
 
             spread_rows(wide_s, pot_s[...])
             row_pass(cache_p, wide_s, HALF, put_wide)
-
-        pb[it, m] = wide[...] - sq_x[...]
-        spread(pb, it, m, *to_m, pb_send, pb_recv)
+            pb[it, m] = wide[...] - sq_x[...]
+            spread(pb, it, m, *to_m, pb_send, pb_recv)
 
         all_of(fb, it, *to_m, fb_send, fb_recv).wait_recv()
         pot_f = -TAU * log_sum(fb[it])
@@ -483,16 +499,15 @@
         gb[it, g] = wide[...] - log_y[...]
         spread(gb, it, g, *to_g, gb_send, gb_recv)
 
-        all_of(pb, it, *to_m, pb_send, pb_recv).wait_recv()
-        new_p = -TAU * log_sum(pb[it])
-        pot_p[...] = 0.5 * (pot_p[...] + new_p)
-
-        @pl.when((it < ITERS - 1) & jnp.logical_not(alone))
-        def _():
-            pots[0, it] = pot_p[half_rows, :]
-            remote(
-                pots.at[0, it], pots.at[1, it], pot_send.at[it], pot_recv.at[it], partner
-            ).start()
+        @pl.when(it == 0)
+        def _():
+            first_pass(lhs_s, rhs_x, cache_p, HALF, put_wide)
+            pb[0, m] = wide[...] - sq_x[...]
+            spread(pb, 0, m, *to_m, pb_send, pb_recv)
+
+        @pl.when(it > 0)
+        def _():
+            finish_p(it)
 
         @pl.when(it == ITERS - 1)
         def _():
@@ -502,7 +517,6 @@
             ).start()
 
         all_of(fb, it, *to_m, fb_send, fb_recv).wait_send()
-        all_of(pb, it, *to_m, pb_send, pb_recv).wait_send()
         all_of(gb, it, *to_g, gb_send, gb_recv).wait_send()
         all_of(gb, it, *to_g, gb_send, gb_recv).wait_recv()
         pot_g = -TAU * log_sum(gb[it])

time: 81.5 us -> 78.9 us (0.968)
  Pallas kernels: 78.8 us -> 76.2 us
    pallas_call x1, Pallas kernels: 74.5 us -> 71.9 us  [on_device(): pl.pallas_call(sinkhorn_kernel, out_shape=(V((32, 128), F32), V((8, 128),...]
where the time goes in v6:
time: 78.9 us; the launch traced here: 78.7 us
  Pallas kernels  76.2 us (97%)
  local copies, waits for them, and re-layouts  1.81 us (2%)
    pallas_call x1, Pallas kernels, on_device(): pl.pallas_call(sinkhorn_kernel, out_shape=(V((32, 128), F32), V((8, 128),...  71.9 us
    pallas_call x1, Pallas kernels, on_device(): pl.pallas_call(relay_kernel, out_shape=jax.ShapeDtypeStruct((4, ROWS, GRO...  4.37 us
    unnamed x3, local copies, waits for them, and re-layouts  1.81 us

profile of v6, /device:TPU:1, one launch (start us, length us, event | category | flops | bytes accessed | tf_op | source)
XLA Modules:
  0.0 78.7 jit_solution(16716469606638840344)
XLA Ops:
  0.6 4.4 %shard_map.94.con_any = f32[4,56,2048]{2,1,0:T(8,128)} custom-call(s32[4]{0:T(128)} %counts_ref.1, f32[50,8192]{1,0:T(8,128)} %feats_any.1, f32[1,8192]{1,0:T(1,128)} %bitcast.10, s32[1,8192]{1,0:T(1,128)} %bitcast.11, f32[32,50]{1,0:T(8,128)} %bitcast.12), custom_call_target="tpu_custom_call" | custom-call | tf_op jit(solution)/shard_map/pallas_call | solution.py:554
  5.0 71.9 %shard_map.95 = (f32[32,128]{1,0:T(8,128)S(1)}, f32[8,128]{1,0:T(8,128)S(1)}, f32[32,128]{1,0:T(8,128)S(1)}) custom-call(f32[4,56,2048]{2,1,0:T(8,128)} %shard_map.94.con_any, f32[50,1024]{1,0:T(8,128)} %tgt_any.1, f32[1,1024]{1,0:T(1,128)} %bitcast.13), custom_call_target="tpu_custom_call" | custom-call | tf_op jit(solution)/shard_map/pallas_call | solution.py:573
  76.9 0.6 copy.13
  77.5 0.6 copy.14
  78.1 0.6 copy.15

commit v7 on v6

--- a/solution.py
+++ b/solution.py
@@ -136,11 +136,18 @@
     return peak + jnp.log2(jnp.sum(jnp.exp2(parts - peak[None]), axis=0))
 
 
+def tree(op, parts):
+    while len(parts) > 1:
+        pairs = [op(a, b) for a, b in zip(parts[0::2], parts[1::2])]
+        parts = pairs + parts[len(pairs) * 2 :]
+    return parts[0]
+
+
 def first_pass(lhs, rhs, cache, count, put, ready=None):
     chunk = min(CHUNK, count)
 
     def both(j, peak):
-        top, total = None, None
+        tops, sums = [], []
         for at in range(0, count, chunk):
             if j < TILES:
                 s = jnp.dot(
@@ -148,15 +155,18 @@
                     preferred_element_type=F32,
                 )
                 cache[j, at : at + chunk, :] = s
-                here = jnp.max(s, axis=0, keepdims=True)
-                top = here if top is None else jnp.maximum(top, here)
+                s = s.reshape(chunk // 8, 8, TILE)
+                tops.append(tree(jnp.maximum, [s[i] for i in range(chunk // 8)]))
             if peak is not None:
-                e = jnp.exp2(cache[j - 1, at : at + chunk, :] - peak)
-                part = jnp.sum(e, axis=0, keepdims=True)
-                total = part if total is None else total + part
+                e = [
+                    jnp.exp2(cache[j - 1, row : row + 8, :] - peak)
+                    for row in range(at, at + chunk, 8)
+                ]
+                sums.append(tree(jnp.add, e))
         if peak is not None:
+            total = jnp.sum(tree(jnp.add, sums), axis=0, keepdims=True)
             put(j - 1, peak + jnp.log2(total))
-        return top
+        return jnp.max(tree(jnp.maximum, tops), axis=0, keepdims=True) if tops else None
 
     peak = None
     for j in range(TILES + 1):
@@ -167,24 +177,22 @@
 
 def row_pass(cache, weight, count, put):
     def body(j, carry):
-        peak, total = [None, None], [None, None]
+        ends = [[], []]
         for at in range(0, count, 128):
-            w = weight[at : at + 128, :]
+            w = [weight[row : row + 8, :] for row in range(at, at + 128, 8)]
             for h in range(2):
-                t = (cache[j, at : at + 128, h * 128 : (h + 1) * 128] + w).reshape(16, 8, 128)
-                top = jnp.max(t, axis=0)
-                if at:
-                    top = jnp.maximum(top, peak[h])
-                part = jnp.sum(jnp.exp2(t - top[None]), axis=0)
-                if at:
-                    part = part + total[h] * jnp.exp2(peak[h] - top)
-                peak[h], total[h] = top, part
-        ends = []
+                lanes = slice(h * 128, (h + 1) * 128)
+                t = [cache[j, at + 8 * i : at + 8 * i + 8, lanes] + w[i] for i in range(16)]
+                top = tree(jnp.maximum, t)
+                ends[h].append((top, tree(jnp.add, [jnp.exp2(v - top) for v in t])))
+        rows = []
         for h in range(2):
-            top = jnp.max(peak[h], axis=0, keepdims=True)
-            part = jnp.sum(total[h] * jnp.exp2(peak[h] - top), axis=0, keepdims=True)
-            ends.append(top + jnp.log2(part))
-        put(j, jnp.concatenate(ends, axis=1))
+            top = tree(jnp.maximum, [v[0] for v in ends[h]])
+            part = tree(jnp.add, [v[1] * jnp.exp2(v[0] - top) for v in ends[h]])
+            most = jnp.max(top, axis=0, keepdims=True)
+            part = jnp.sum(part * jnp.exp2(top - most), axis=0, keepdims=True)
+            rows.append(most + jnp.log2(part))
+        put(j, jnp.concatenate(rows, axis=1))
         return carry
 
     lax.fori_loop(0, TILES, body, 0)
@@ -202,14 +210,10 @@
                 lanes = slice(r % 2 * 128, r % 2 * 128 + 128)
                 t = cache[r // 2, rows, lanes].reshape(2, 8, 128)
                 parts.append(t + spread_w[r][None])
-            tops = parts
-            while len(tops) > 1:
-                tops = [jnp.maximum(a, b) for a, b in zip(tops[0::2], tops[1::2])]
-            sums = [jnp.exp2(t - tops[0]) for t in parts]
-            while len(sums) > 1:
-                sums = [a + b for a, b in zip(sums[0::2], sums[1::2])]
-            peaks[rows, :] = tops[0].reshape(16, 128)
-            totals[rows, :] = sums[0].reshape(16, 128)
+            top = tree(jnp.maximum, parts)
+            total = tree(jnp.add, [jnp.exp2(t - top) for t in parts])
+            peaks[rows, :] = top.reshape(16, 128)
+            totals[rows, :] = total.reshape(16, 128)
         return carry
 
     lax.fori_loop(0, GROUP // 128, body, 0)

time: 78.9 us -> 79.2 us (level)
  no operation moved by 1% of the time
where the time goes in v7:
time: 79.2 us; the launch traced here: 79.1 us
  Pallas kernels  76.6 us (97%)
  local copies, waits for them, and re-layouts  1.81 us (2%)
    pallas_call x1, Pallas kernels, on_device(): pl.pallas_call(sinkhorn_kernel, out_shape=(V((32, 128), F32), V((8, 128),...  72.2 us
    pallas_call x1, Pallas kernels, on_device(): pl.pallas_call(relay_kernel, out_shape=jax.ShapeDtypeStruct((4, ROWS, GRO...  4.37 us
    unnamed x3, local copies, waits for them, and re-layouts  1.81 us

profile of v7, /device:TPU:1, one launch (start us, length us, event | category | flops | bytes accessed | tf_op | source)
XLA Modules:
  0.0 79.1 jit_solution(14228020785597512807)
XLA Ops:
  0.6 4.4 %shard_map.94.con_any = f32[4,56,2048]{2,1,0:T(8,128)} custom-call(s32[4]{0:T(128)} %counts_ref.1, f32[50,8192]{1,0:T(8,128)} %feats_any.1, f32[1,8192]{1,0:T(1,128)} %bitcast.10, s32[1,8192]{1,0:T(1,128)} %bitcast.11, f32[32,50]{1,0:T(8,128)} %bitcast.12), custom_call_target="tpu_custom_call" | custom-call | tf_op jit(solution)/shard_map/pallas_call | solution.py:558
  5.0 72.2 %shard_map.95 = (f32[32,128]{1,0:T(8,128)S(1)}, f32[8,128]{1,0:T(8,128)S(1)}, f32[32,128]{1,0:T(8,128)S(1)}) custom-call(f32[4,56,2048]{2,1,0:T(8,128)} %shard_map.94.con_any, f32[50,1024]{1,0:T(8,128)} %tgt_any.1, f32[1,1024]{1,0:T(1,128)} %bitcast.13), custom_call_target="tpu_custom_call" | custom-call | tf_op jit(solution)/shard_map/pallas_call | solution.py:577
  77.3 0.6 copy.13
  77.9 0.6 copy.14
  78.5 0.6 copy.15

commit v8 on v7

--- a/solution.py
+++ b/solution.py
@@ -175,10 +175,10 @@
         peak = both(j, peak)
 
 
-def row_pass(cache, weight, count, put):
+def row_pass(cache, weight, span, tiles, state, begin, end, put):
     def body(j, carry):
         ends = [[], []]
-        for at in range(0, count, 128):
+        for at in range(span[0], span[1], 128):
             w = [weight[row : row + 8, :] for row in range(at, at + 128, 8)]
             for h in range(2):
                 lanes = slice(h * 128, (h + 1) * 128)
@@ -187,37 +187,53 @@
                 ends[h].append((top, tree(jnp.add, [jnp.exp2(v - top) for v in t])))
         rows = []
         for h in range(2):
+            lanes = slice(h * 128, (h + 1) * 128)
+            if not begin:
+                ends[h].append((state[0, j, :, lanes], state[1, j, :, lanes]))
             top = tree(jnp.maximum, [v[0] for v in ends[h]])
             part = tree(jnp.add, [v[1] * jnp.exp2(v[0] - top) for v in ends[h]])
-            most = jnp.max(top, axis=0, keepdims=True)
-            part = jnp.sum(part * jnp.exp2(top - most), axis=0, keepdims=True)
-            rows.append(most + jnp.log2(part))
-        put(j, jnp.concatenate(rows, axis=1))
+            if end:
+                most = jnp.max(top, axis=0, keepdims=True)
+                part = jnp.sum(part * jnp.exp2(top - most), axis=0, keepdims=True)
+                rows.append(most + jnp.log2(part))
+            else:
+                state[0, j, :, lanes] = top
+                state[1, j, :, lanes] = part
+        if end:
+            put(j, jnp.concatenate(rows, axis=1))
         return carry
 
-    lax.fori_loop(0, TILES, body, 0)
-
-
-def column_pass(cache, weight, spread_w, peaks, totals, out):
-    for r in range(16):
+    lax.fori_loop(tiles[0], tiles[1], body, 0)
+
+
+def column_pass(cache, weight, half, blocks, spread_w, peaks, totals):
+    for r in range(8):
         spread_w[r] = jnp.broadcast_to(weight[r : r + 1, :], (8, 128))
 
     def body(block, carry):
-        for sub in range(8):
-            rows = pl.ds(pl.multiple_of(block * 128 + sub * 16, 16), 16)
+        for sub in range(4):
+            rows = pl.ds(pl.multiple_of(block * 128 + sub * 32, 32), 32)
             parts = []
-            for r in range(16):
+            for r in range(8):
                 lanes = slice(r % 2 * 128, r % 2 * 128 + 128)
-                t = cache[r // 2, rows, lanes].reshape(2, 8, 128)
+                t = cache[half * 4 + r // 2, rows, lanes].reshape(4, 8, 128)
                 parts.append(t + spread_w[r][None])
             top = tree(jnp.maximum, parts)
-            total = tree(jnp.add, [jnp.exp2(t - top) for t in parts])
-            peaks[rows, :] = top.reshape(16, 128)
-            totals[rows, :] = total.reshape(16, 128)
+            if half:
+                before = peaks[rows, :].reshape(4, 8, 128)
+                top = jnp.maximum(top, before)
+            sums = [jnp.exp2(t - top) for t in parts]
+            if half:
+                sums.append(totals[rows, :].reshape(4, 8, 128) * jnp.exp2(before - top))
+            peaks[rows, :] = top.reshape(32, 128)
+            totals[rows, :] = tree(jnp.add, sums).reshape(32, 128)
         return carry
 
-    lax.fori_loop(0, GROUP // 128, body, 0)
-    for c in range(16):
+    lax.fori_loop(blocks[0], blocks[1], body, 0)
+
+
+def over_lanes(peaks, totals, blocks, out):
+    for c in range(blocks[0], blocks[1]):
         at = slice(c * 128, (c + 1) * 128)
         turned = peaks[at, :].T
         top = jnp.max(turned, axis=0, keepdims=True)
@@ -225,9 +241,10 @@
         out[c : c + 1, :] = top + jnp.log2(total)
 
 
-def spread_rows(wide_w, weight):
+def spread_rows(wide_w, weight, first=0):
     for c in range(weight.shape[0]):
-        wide_w[c * 128 : (c + 1) * 128, :] = jnp.broadcast_to(weight[c : c + 1, :], (128, 128)).T
+        at = slice((first + c) * 128, (first + c + 1) * 128)
+        wide_w[at, :] = jnp.broadcast_to(weight[c : c + 1, :], (128, 128)).T
 
 
 def to_rows(ref, row, first=0):
@@ -276,8 +293,8 @@
     con_ref, tgt_ref, tgt_mass_ref,
     from_own, from_opp, opp, landed, ybuf, xfull, sbuf,
     lhs_y, lhs_s, fix_y, fix_s, rhs_x, cache_f, cache_p,
-    spread_w, peaks, totals, wide_g, wide_s,
-    sq_x, sq_y, sq_s, log_x, log_y, log_s, pot_p, pot_s, wide,
+    spread_w, peaks, totals, wide_g, wide_s, state, gwide,
+    sq_x, sq_y, sq_s, log_x, log_y, log_s, pot_p, pot_s, wide, pots_f,
     fb, pb, gb, pots, fin,
     relay_send, relay_recv, opp_send, opp_recv, own_sem, tgt_sem, self_sem, local_sem,
     fb_send, fb_recv, pb_send, pb_recv,
@@ -405,26 +422,59 @@
         high, middle, unused = pieces(kept * (2.0 * SCALE))
         set_right(rhs_x, s, high, middle, high)
 
-    first_pass(lhs_y, rhs_x, cache_f, GROUP, put_wide, arrive)
+    def spread(at, me, others, peer, send, recv):
+        for k in others:
+            remote(at.at[me], at.at[me], send, recv, peer(k)).start()
+
+    def all_of(at, others, peer, send, recv):
+        part = at.at[pl.ds(0, len(others))]
+        return remote(part, part, send, recv, peer(others[0]))
+
+    to_m, to_g = (m_others, m_peer), (g_others, g_peer)
+
+    def f_box(it, n):
+        return fb.at[it, n], fb_send.at[it, n], fb_recv.at[it, n]
+
+    def g_box(it, n):
+        return gb.at[it, n], gb_send.at[it, n], gb_recv.at[it, n]
+
+    def p_box(it):
+        return pb.at[it], pb_send.at[it], pb_recv.at[it]
+
+    def send_f(it, n):
+        at, send, recv = f_box(it, n)
+        rows = slice(8 * n, 8 * n + 8)
+        at[m] = wide[rows, :] - sq_x[rows, :]
+        spread(at, m, *to_m, send, recv)
+
+    def send_p(it):
+        at, send, recv = p_box(it)
+        at[m] = wide[...] - sq_x[...]
+        spread(at, m, *to_m, send, recv)
+
+    def send_g(it, n):
+        at, send, recv = g_box(it, n)
+        rows = slice(8 * n, 8 * n + 8)
+        at[g] = gwide[rows, :] - log_y[rows, :]
+        spread(at, g, *to_g, send, recv)
+
+    def put_first(j, value):
+        put_wide(j, value)
+        if j % 4 == 3:
+            send_f(0, j // 4)
+
+    first_pass(lhs_y, rhs_x, cache_f, GROUP, put_first, arrive)
 
     pot_p[...] = jnp.zeros_like(pot_p)
     pot_s[...] = jnp.zeros_like(pot_s)
 
-    def spread(box, it, me, others, peer, send, recv):
-        for k in others:
-            remote(box.at[it, me], box.at[it, me], send.at[it], recv.at[it], peer(k)).start()
-
-    def all_of(box, it, others, peer, send, recv):
-        part = box.at[it, pl.ds(0, len(others))]
-        return remote(part, part, send.at[it], recv.at[it], peer(others[0]))
-
-    to_m, to_g = (m_others, m_peer), (g_others, g_peer)
-
     half_rows = pl.ds(pl.multiple_of(x_hi * 8, 8), 8)
 
     def finish_p(it):
-        all_of(pb, it, *to_m, pb_send, pb_recv).wait_recv()
-        all_of(pb, it, *to_m, pb_send, pb_recv).wait_send()
+        at, send, recv = p_box(it)
+        moved = all_of(at, *to_m, send, recv)
+        moved.wait_recv()
+        moved.wait_send()
         pot_p[...] = 0.5 * (pot_p[...] - TAU * log_sum(pb[it]))
 
         @pl.when((it < ITERS - 1) & jnp.logical_not(alone))
@@ -437,10 +487,18 @@
     def iteration(it, carry):
         @pl.when(it > 0)
         def _():
-            row_pass(cache_f, wide_g, GROUP, put_wide)
-
-        fb[it, m] = wide[...] - sq_x[...]
-        spread(fb, it, m, *to_m, fb_send, fb_recv)
+            for n in range(2):
+                at, send, recv = g_box(it - 1, n)
+                moved = all_of(at, *to_g, send, recv)
+                moved.wait_recv()
+                spread_rows(wide_g, -TAU * log_sum(at[...]), 8 * n)
+                if n == 0:
+                    row_pass(cache_f, wide_g, (0, HALF), (0, 8), state, True, False, None)
+                moved.wait_send()
+            for n in range(2):
+                tiles = (4 * n, 4 * n + 4)
+                row_pass(cache_f, wide_g, (HALF, GROUP), tiles, state, False, True, put_wide)
+                send_f(it, n)
 
         @pl.when(it == 0)
         def _():
@@ -486,28 +544,37 @@
                 pot_s[...] = pots[1, last]
 
             spread_rows(wide_s, pot_s[...])
-            row_pass(cache_p, wide_s, HALF, put_wide)
-            pb[it, m] = wide[...] - sq_x[...]
-            spread(pb, it, m, *to_m, pb_send, pb_recv)
-
-        all_of(fb, it, *to_m, fb_send, fb_recv).wait_recv()
-        pot_f = -TAU * log_sum(fb[it])
+            row_pass(cache_p, wide_s, (0, HALF), (0, 8), None, True, True, put_wide)
+            send_p(it)
+
+        sent = []
+        for n in range(2):
+            at, send, recv = f_box(it, n)
+            sent.append(all_of(at, *to_m, send, recv))
+            sent[n].wait_recv()
+            rows = slice(8 * n, 8 * n + 8)
+            pot_f = -TAU * log_sum(at[...])
+            pots_f[rows, :] = pot_f
+            weight = log_x[rows, :] + pot_f - sq_x[rows, :]
+            if n == 0:
+                column_pass(cache_f, weight, 0, (0, 16), spread_w, peaks, totals)
+        for n in range(2):
+            blocks = (8 * n, 8 * n + 8)
+            column_pass(cache_f, weight, 1, blocks, spread_w, peaks, totals)
+            over_lanes(peaks, totals, blocks, gwide)
+            send_g(it, n)
+
         @pl.when(it == ITERS - 1)
         def _():
-            fin[0, z_lo] = pot_f * (1.0 / SCALE)
+            fin[0, z_lo] = pots_f[...] * (1.0 / SCALE)
             remote(
                 fin.at[0, z_lo], fin.at[0, z_lo], fin_send.at[0], fin_recv.at[0], twin
             ).start()
 
-        column_pass(cache_f, log_x[...] + pot_f - sq_x[...], spread_w, peaks, totals, wide)
-        gb[it, g] = wide[...] - log_y[...]
-        spread(gb, it, g, *to_g, gb_send, gb_recv)
-
         @pl.when(it == 0)
         def _():
             first_pass(lhs_s, rhs_x, cache_p, HALF, put_wide)
-            pb[0, m] = wide[...] - sq_x[...]
-            spread(pb, 0, m, *to_m, pb_send, pb_recv)
+            send_p(0)
 
         @pl.when(it > 0)
         def _():
@@ -520,21 +587,18 @@
                 fin.at[1, z_lo], fin.at[1, z_lo], fin_send.at[1], fin_recv.at[1], twin
             ).start()
 
-        all_of(fb, it, *to_m, fb_send, fb_recv).wait_send()
-        all_of(gb, it, *to_g, gb_send, gb_recv).wait_send()
-        all_of(gb, it, *to_g, gb_send, gb_recv).wait_recv()
-        pot_g = -TAU * log_sum(gb[it])
-        wide[...] = pot_g
-
-        @pl.when(it < ITERS - 1)
-        def _():
-            spread_rows(wide_g, pot_g)
-
+        for copy in sent:
+            copy.wait_send()
         return carry
 
     lax.fori_loop(0, ITERS, iteration, 0)
 
-    tgt_out[...] = wide[pl.ds(pl.multiple_of(z_lo * 8, 8), 8), :] * (1.0 / SCALE)
+    for n in range(2):
+        at, send, recv = g_box(ITERS - 1, n)
+        moved = all_of(at, *to_g, send, recv)
+        moved.wait_recv()
+        moved.wait_send()
+    tgt_out[...] = (-TAU / SCALE) * log_sum(gb[ITERS - 1, z_lo])
     for kind in range(2):
         remote(
             fin.at[kind, 1 - z_lo], fin.at[kind, 1 - z_lo], fin_send.at[kind], fin_recv.at[kind],
@@ -589,16 +653,16 @@
             V((GROUP, 256), BF16), V((HALF, 256), BF16),
             V((GROUP, 128), BF16), V((HALF, 128), BF16), V((256, GROUP), BF16),
             V((TILES, GROUP, TILE), F32), V((TILES, HALF, TILE), F32),
-            V((16, 8, 128), F32), V((GROUP, 128), F32), V((GROUP, 128), F32),
-            V((GROUP, 128), F32), V((HALF, 128), F32),
+            V((8, 8, 128), F32), V((GROUP, 128), F32), V((GROUP, 128), F32),
+            V((GROUP, 128), F32), V((HALF, 128), F32), V((2, TILES, 8, TILE), F32), V(rows16, F32),
             V(rows16, F32), V(rows16, F32), V(rows8, F32),
             V(rows16, F32), V(rows16, F32), V(rows8, F32),
-            V(rows16, F32), V(rows8, F32), V(rows16, F32),
-            V((ITERS, 16) + rows16, F32), V((ITERS, 16) + rows16, F32),
-            V((ITERS, 8) + rows16, F32), V((2, ITERS - 1) + rows8, F32),
+            V(rows16, F32), V(rows8, F32), V(rows16, F32), V(rows16, F32),
+            V((ITERS, 2, 16) + rows8, F32), V((ITERS, 16) + rows16, F32),
+            V((ITERS, 2, 8) + rows8, F32), V((2, ITERS - 1) + rows8, F32),
             V((2, 2) + rows16, F32),
             D((4,)), D((4,)), D((4,)), D((4,)), D((2,)), D((2,)), D((2,)), D,
-            D((ITERS,)), D((ITERS,)), D((ITERS,)), D((ITERS,)), D((ITERS,)), D((ITERS,)),
+            D((ITERS, 2)), D((ITERS, 2)), D((ITERS,)), D((ITERS,)), D((ITERS, 2)), D((ITERS, 2)),
             D((ITERS,)), D((ITERS,)), D((2,)), D((2,)),
             D((4,)),
         ],

time: 79.2 us -> 76.5 us (0.966)
  Pallas kernels: 76.6 us -> 73.9 us
    pallas_call x1, Pallas kernels: 72.2 us -> 69.5 us  [on_device(): pl.pallas_call(sinkhorn_kernel, out_shape=(V((32, 128), F32), V((8, 128),...]
where the time goes in v8:
time: 76.5 us; the launch traced here: 76.4 us
  Pallas kernels  73.9 us (97%)
  local copies, waits for them, and re-layouts  1.81 us (2%)
    pallas_call x1, Pallas kernels, on_device(): pl.pallas_call(sinkhorn_kernel, out_shape=(V((32, 128), F32), V((8, 128),...  69.5 us
    pallas_call x1, Pallas kernels, on_device(): pl.pallas_call(relay_kernel, out_shape=jax.ShapeDtypeStruct((4, ROWS, GRO...  4.37 us
    unnamed x3, local copies, waits for them, and re-layouts  1.81 us

profile of v8, /device:TPU:1, one launch (start us, length us, event | category | flops | bytes accessed | tf_op | source)
XLA Modules:
  0.0 76.4 jit_solution(16097210817207771234)
XLA Ops:
  0.6 4.4 %shard_map.94.con_any = f32[4,56,2048]{2,1,0:T(8,128)} custom-call(s32[4]{0:T(128)} %counts_ref.1, f32[50,8192]{1,0:T(8,128)} %feats_any.1, f32[1,8192]{1,0:T(1,128)} %bitcast.10, s32[1,8192]{1,0:T(1,128)} %bitcast.11, f32[32,50]{1,0:T(8,128)} %bitcast.12), custom_call_target="tpu_custom_call" | custom-call | tf_op jit(solution)/shard_map/pallas_call | solution.py:622
  5.0 69.5 %shard_map.95 = (f32[32,128]{1,0:T(8,128)S(1)}, f32[8,128]{1,0:T(8,128)S(1)}, f32[32,128]{1,0:T(8,128)S(1)}) custom-call(f32[4,56,2048]{2,1,0:T(8,128)} %shard_map.94.con_any, f32[50,1024]{1,0:T(8,128)} %tgt_any.1, f32[1,1024]{1,0:T(1,128)} %bitcast.13), custom_call_target="tpu_custom_call" | custom-call | tf_op jit(solution)/shard_map/pallas_call | solution.py:641
  74.6 0.6 copy.13
  75.2 0.6 copy.14
  75.8 0.6 copy.15

commit v9 on v8

--- a/solution.py
+++ b/solution.py
@@ -58,7 +58,7 @@
     for at in range(0, CAP, 1024):
         ready(at)
         ids = ids_ref[:, at : at + 1024]
-        section = lax.rem(lax.broadcasted_iota(jnp.int32, (3 * SECTIONS, 1024), 0), SECTIONS)
+        section = lax.broadcasted_iota(jnp.int32, (3 * SECTIONS, 1024), 0) & (SECTIONS - 1)
         onehot = jnp.where(section == ids, 1.0, 0.0).astype(BF16)
         shift = lax.dot_general(
             three, onehot, (((0,), (0,)), ((), ())), preferred_element_type=F32
@@ -252,32 +252,29 @@
         ref[first + r : first + r + 1, :] = row[:, r * 128 : (r + 1) * 128]
 
 
-def set_weights(lhs, fixed, weight):
+def block_rows(first, c):
+    return pl.ds(pl.multiple_of(first + c * 128, 128), 128)
+
+
+def set_left(lhs, first, one, two, three, weight):
     rows = weight.shape[0]
     parts = [p.astype(F32) for p in pieces(weight)]
-    stacked = jnp.concatenate(parts + [jnp.zeros((128 - 3 * rows, 128), F32)], axis=0)
-    turned = stacked.T
-    lane = lax.rem(lax.broadcasted_iota(jnp.int32, (128, 128), 1), rows)
+    fill = jnp.zeros((64 - 3 * rows, 128), F32)
     for c in range(rows):
         at = slice(c * 128, (c + 1) * 128)
-        lhs[at, 128:256] = jnp.where(lane == c, turned, 0.0).astype(BF16) + fixed[at, :]
-
-
-def set_left(lhs, fixed, one, two, three):
-    zero = jnp.zeros((64, 128), F32)
-    for c in range(one.shape[1] // 128):
-        at = slice(c * 128, (c + 1) * 128)
-        first = jnp.concatenate([one[:, at].astype(F32), two[:, at].astype(F32)], axis=0)
-        second = jnp.concatenate([zero, three[:, at].astype(F32)], axis=0)
-        lhs[at, 0:128] = first.T.astype(BF16)
-        fixed[at, :] = second.T.astype(BF16)
+        upper = jnp.concatenate([one[:, at].astype(F32), two[:, at].astype(F32)], axis=0)
+        row = lax.broadcasted_iota(jnp.int32, (rows, 128), 0)
+        chosen = [jnp.where(row == c, p, 0.0) for p in parts]
+        lower = jnp.concatenate(chosen + [fill, three[:, at].astype(F32)], axis=0)
+        lhs[block_rows(first, c), 0:128] = upper.T.astype(BF16)
+        lhs[block_rows(first, c), 128:256] = lower.T.astype(BF16)
 
 
 def set_right(rhs, at, one, two, three):
     rhs[0:64, at] = one
     rhs[64:128, at] = two
     row = lax.broadcasted_iota(jnp.int32, three.shape, 0)
-    rhs[128:192, at] = jnp.where(row < 48, 1.0, 0.0).astype(BF16)
+    rhs[128:192, at] = jnp.where(row < 24, 1.0, 0.0).astype(BF16)
     rhs[192:256, at] = three
 
 
@@ -292,9 +289,9 @@
     src_out, tgt_out, self_out,
     con_ref, tgt_ref, tgt_mass_ref,
     from_own, from_opp, opp, landed, ybuf, xfull, sbuf,
-    lhs_y, lhs_s, fix_y, fix_s, rhs_x, cache_f, cache_p,
+    lhs_y, lhs_s, rhs_x, cache_f, cache_p,
     spread_w, peaks, totals, wide_g, wide_s, state, gwide,
-    sq_x, sq_y, sq_s, log_x, log_y, log_s, pot_p, pot_s, wide, pots_f,
+    sq_x, sq_s, log_x, log_y, log_s, pot_p, pot_s, wide, pots_f,
     fb, pb, gb, pots, fin,
     relay_send, relay_recv, opp_send, opp_recv, own_sem, tgt_sem, self_sem, local_sem,
     fb_send, fb_recv, pb_send, pb_recv,
@@ -362,8 +359,12 @@
         for c, s in enumerate(parts)
     ]
     own = remote(con_any.at[1], from_own, own_sem.at[0], own_sem.at[1], sibling)
-    tgt = remote(ybuf.at[z_lo], ybuf.at[z_lo], tgt_sem.at[0], tgt_sem.at[1], twin)
+    quarter = pl.ds(pl.multiple_of(core * 512, 512), 512)
+    rest = pl.ds(pl.multiple_of((1 - core) * 512, 512), 512)
+    here, there = ybuf.at[z_lo, :, quarter], ybuf.at[1 - z_lo, :, quarter]
+    tgt = remote(here, here, tgt_sem.at[0], tgt_sem.at[1], twin)
     tgt.start()
+    passed = remote(there, there, tgt_sem.at[2], tgt_sem.at[3], sibling)
 
     for copy in relays:
         copy.start()
@@ -372,21 +373,33 @@
         remote(opp.at[:, s], landed.at[:, s], opp_send.at[c], opp_recv.at[c], opposite)
         for c, s in enumerate(parts)
     ]
+
+    def target(part, centre):
+        first, at = part * HALF, pl.ds(pl.multiple_of(part * 8, 8), 8)
+        cells = ybuf[part]
+        kept = padded(cells, centre)
+        square = jnp.sum(kept * kept, axis=0, keepdims=True) * SCALE
+        mass = jnp.log2(cells[COMPONENTS : COMPONENTS + 1, :])
+        log_y[at, :] = jnp.concatenate([mass[:, r * 128 : (r + 1) * 128] for r in range(8)], axis=0)
+        square = jnp.concatenate([square[:, r * 128 : (r + 1) * 128] for r in range(8)], axis=0)
+        high, middle, unused = pieces(kept)
+        set_left(lhs_y, first, high, high, middle, log_y[at, :] - square)
+
+    def pass_on(c):
+        relays[c].wait_recv()
+        opp[:, parts[c]] = con_ref[1, :, parts[c]] + from_opp[:, parts[c]]
+        onward[c].start()
+
+    centre = jnp.sum(ybuf[z_lo], axis=1, keepdims=True) * (1.0 / HALF)
     loads[2].wait()
-    for c, s in enumerate(parts):
-        relays[c].wait_recv()
-        opp[:, s] = con_ref[1, :, s] + from_opp[:, s]
-        onward[c].start()
-
-    remote(ybuf.at[1 - z_lo], ybuf.at[1 - z_lo], tgt_sem.at[0], tgt_sem.at[1], twin).wait_recv()
-    cells = jnp.concatenate([ybuf[0], ybuf[1]], axis=1)
-    centre = jnp.sum(cells, axis=1, keepdims=True) * (1.0 / GROUP)
-    kept = padded(cells, centre)
-    to_rows(sq_y, jnp.sum(kept * kept, axis=0, keepdims=True) * SCALE)
-    to_rows(log_y, jnp.log2(cells[COMPONENTS : COMPONENTS + 1, :]))
-    high, middle, unused = pieces(kept)
-    set_left(lhs_y, fix_y, high, high, middle)
-    set_weights(lhs_y, fix_y, log_y[...] - sq_y[...])
+    for c in range(4):
+        pass_on(c)
+    target(z_lo, centre)
+    remote(there, there, tgt_sem.at[0], tgt_sem.at[1], twin).wait_recv()
+    passed.start()
+    handed = ybuf.at[1 - z_lo, :, rest]
+    remote(handed, handed, tgt_sem.at[2], tgt_sem.at[3], sibling).wait_recv()
+    target(1 - z_lo, centre)
 
     def put_wide(j, value):
         for r in range(TILE // 128):
@@ -511,15 +524,14 @@
                 shared.wait_recv()
                 shared.wait_send()
 
-            for copy in relays + onward + [own, tgt]:
+            for copy in relays + onward + [own, tgt, passed]:
                 copy.wait_send()
             got = sbuf[...]
             columns = padded(got, centre)
             to_rows(sq_s, jnp.sum(columns * columns, axis=0, keepdims=True) * SCALE)
             to_rows(log_s, jnp.log2(got[COMPONENTS : COMPONENTS + 1, :]))
             upper, lower, unused = pieces(columns)
-            set_left(lhs_s, fix_s, upper, upper, lower)
-            set_weights(lhs_s, fix_s, log_s[...] - sq_s[...])
+            set_left(lhs_s, 0, upper, upper, lower, log_s[...] - sq_s[...])
 
         @pl.when(it == 1)
         def _():
@@ -651,17 +663,16 @@
             V((ROWS, GROUP), F32), V((2, ROWS, HALF), F32), V((ROWS, GROUP), F32),
             V((ROWS, HALF), F32),
             V((GROUP, 256), BF16), V((HALF, 256), BF16),
-            V((GROUP, 128), BF16), V((HALF, 128), BF16), V((256, GROUP), BF16),
+            V((256, GROUP), BF16),
             V((TILES, GROUP, TILE), F32), V((TILES, HALF, TILE), F32),
             V((8, 8, 128), F32), V((GROUP, 128), F32), V((GROUP, 128), F32),
             V((GROUP, 128), F32), V((HALF, 128), F32), V((2, TILES, 8, TILE), F32), V(rows16, F32),
-            V(rows16, F32), V(rows16, F32), V(rows8, F32),
-            V(rows16, F32), V(rows16, F32), V(rows8, F32),
+            V(rows16, F32), V(rows8, F32), V(rows16, F32), V(rows16, F32), V(rows8, F32),
             V(rows16, F32), V(rows8, F32), V(rows16, F32), V(rows16, F32),
             V((ITERS, 2, 16) + rows8, F32), V((ITERS, 16) + rows16, F32),
             V((ITERS, 2, 8) + rows8, F32), V((2, ITERS - 1) + rows8, F32),
             V((2, 2) + rows16, F32),
-            D((4,)), D((4,)), D((4,)), D((4,)), D((2,)), D((2,)), D((2,)), D,
+            D((4,)), D((4,)), D((4,)), D((4,)), D((2,)), D((4,)), D((2,)), D,
             D((ITERS, 2)), D((ITERS, 2)), D((ITERS,)), D((ITERS,)), D((ITERS, 2)), D((ITERS, 2)),
             D((ITERS,)), D((ITERS,)), D((2,)), D((2,)),
             D((4,)),

time: 76.5 us -> 74.7 us (0.976)
  Pallas kernels: 73.9 us -> 72.1 us
    pallas_call x1, Pallas kernels: 69.5 us -> 67.7 us  [on_device(): pl.pallas_call(sinkhorn_kernel, out_shape=(V((32, 128), F32), V((8, 128),...]
where the time goes in v9:
time: 74.7 us; the launch traced here: 74.5 us
  Pallas kernels  72.1 us (97%)
  local copies, waits for them, and re-layouts  1.81 us (2%)
    pallas_call x1, Pallas kernels, on_device(): pl.pallas_call(sinkhorn_kernel, out_shape=(V((32, 128), F32), V((8, 128),...  67.7 us
    pallas_call x1, Pallas kernels, on_device(): pl.pallas_call(relay_kernel, out_shape=jax.ShapeDtypeStruct((4, ROWS, GRO...  4.37 us
    unnamed x3, local copies, waits for them, and re-layouts  1.81 us

profile of v9, /device:TPU:1, one launch (start us, length us, event | category | flops | bytes accessed | tf_op | source)
XLA Modules:
  0.0 74.5 jit_solution(2521948077461003371)
XLA Ops:
  0.6 4.4 %shard_map.94.con_any = f32[4,56,2048]{2,1,0:T(8,128)} custom-call(s32[4]{0:T(128)} %counts_ref.1, f32[50,8192]{1,0:T(8,128)} %feats_any.1, f32[1,8192]{1,0:T(1,128)} %bitcast.10, s32[1,8192]{1,0:T(1,128)} %bitcast.11, f32[32,50]{1,0:T(8,128)} %bitcast.12), custom_call_target="tpu_custom_call" | custom-call | tf_op jit(solution)/shard_map/pallas_call | solution.py:634
  5.0 67.7 %shard_map.95 = (f32[32,128]{1,0:T(8,128)S(1)}, f32[8,128]{1,0:T(8,128)S(1)}, f32[32,128]{1,0:T(8,128)S(1)}) custom-call(f32[4,56,2048]{2,1,0:T(8,128)} %shard_map.94.con_any, f32[50,1024]{1,0:T(8,128)} %tgt_any.1, f32[1,1024]{1,0:T(1,128)} %bitcast.13), custom_call_target="tpu_custom_call" | custom-call | tf_op jit(solution)/shard_map/pallas_call | solution.py:653
  72.7 0.6 copy.13
  73.3 0.6 copy.14
  73.9 0.6 copy.15

commit v10 on v9

--- a/solution.py
+++ b/solution.py
@@ -87,8 +87,8 @@
 
 
 def relay_kernel(
-    counts_ref, feats_any, mass_any, ids_any, offsets_any, out_any,
-    held, feats_ref, mass_ref, ids_ref, offsets_ref, out_ref, feats_sem, small_sem, out_sem,
+    counts_ref, feats_any, mass_any, ids_any, offsets_any, out_ref,
+    held, feats_ref, mass_ref, ids_ref, offsets_ref, feats_sem, small_sem,
 ):
     small = [
         pltpu.make_async_copy(a, b, small_sem.at[i])
@@ -118,17 +118,10 @@
     for copy in small:
         copy.wait()
     correct(feats_ref, mass_ref, ids_ref, offsets_ref, held, ready)
-    moves = []
-    for index in (3, 2, 1, 0):
+    for index in range(4):
         to_x, to_core = lax.rem(x_lo + index // 2, 2), lax.rem(core + index % 2, 2)
         base = (to_x * 2 + to_core) * (2 * GROUP) + z_lo * GROUP - begin
         contribute(held, base, count, out_ref.at[index])
-        moves.append(
-            pltpu.make_async_copy(out_ref.at[index], out_any.at[index], out_sem.at[index])
-        )
-        moves[-1].start()
-    for copy in moves:
-        copy.wait()
 
 
 def log_sum(parts):
@@ -175,8 +168,17 @@
         peak = both(j, peak)
 
 
+def several(body, span, each):
+    def turn(i, carry):
+        for k in range(each):
+            body(i * each + k)
+        return carry
+
+    lax.fori_loop(span[0] // each, span[1] // each, turn, 0)
+
+
 def row_pass(cache, weight, span, tiles, state, begin, end, put):
-    def body(j, carry):
+    def body(j):
         ends = [[], []]
         for at in range(span[0], span[1], 128):
             w = [weight[row : row + 8, :] for row in range(at, at + 128, 8)]
@@ -201,16 +203,15 @@
                 state[1, j, :, lanes] = part
         if end:
             put(j, jnp.concatenate(rows, axis=1))
-        return carry
-
-    lax.fori_loop(tiles[0], tiles[1], body, 0)
+
+    several(body, tiles, 2)
 
 
 def column_pass(cache, weight, half, blocks, spread_w, peaks, totals):
     for r in range(8):
         spread_w[r] = jnp.broadcast_to(weight[r : r + 1, :], (8, 128))
 
-    def body(block, carry):
+    def body(block):
         for sub in range(4):
             rows = pl.ds(pl.multiple_of(block * 128 + sub * 32, 32), 32)
             parts = []
@@ -227,9 +228,8 @@
                 sums.append(totals[rows, :].reshape(4, 8, 128) * jnp.exp2(before - top))
             peaks[rows, :] = top.reshape(32, 128)
             totals[rows, :] = tree(jnp.add, sums).reshape(32, 128)
-        return carry
-
-    lax.fori_loop(blocks[0], blocks[1], body, 0)
+
+    several(body, blocks, 4)
 
 
 def over_lanes(peaks, totals, blocks, out):
@@ -285,9 +285,9 @@
 
 
 def sinkhorn_kernel(
-    con_any, tgt_any, tgt_mass_any,
+    con_ref, tgt_any, tgt_mass_any,
     src_out, tgt_out, self_out,
-    con_ref, tgt_ref, tgt_mass_ref,
+    tgt_ref, tgt_mass_ref,
     from_own, from_opp, opp, landed, ybuf, xfull, sbuf,
     lhs_y, lhs_s, rhs_x, cache_f, cache_p,
     spread_w, peaks, totals, wide_g, wide_s, state, gwide,
@@ -329,12 +329,7 @@
     loads = [
         pltpu.make_async_copy(a, b, con_sem.at[i])
         for i, (a, b) in enumerate(
-            [
-                (tgt_any, tgt_ref),
-                (tgt_mass_any, tgt_mass_ref),
-                (con_any.at[2], con_ref.at[1]),
-                (con_any.at[0], con_ref.at[0]),
-            ]
+            [(tgt_any, tgt_ref), (tgt_mass_any, tgt_mass_ref)]
         )
     ]
     for copy in loads:
@@ -355,10 +350,10 @@
 
     parts = [slice(c * 512, (c + 1) * 512) for c in range(4)]
     relays = [
-        remote(con_any.at[3, :, s], from_opp.at[:, s], relay_send.at[c], relay_recv.at[c], sibling)
+        remote(con_ref.at[3, :, s], from_opp.at[:, s], relay_send.at[c], relay_recv.at[c], sibling)
         for c, s in enumerate(parts)
     ]
-    own = remote(con_any.at[1], from_own, own_sem.at[0], own_sem.at[1], sibling)
+    own = remote(con_ref.at[1], from_own, own_sem.at[0], own_sem.at[1], sibling)
     quarter = pl.ds(pl.multiple_of(core * 512, 512), 512)
     rest = pl.ds(pl.multiple_of((1 - core) * 512, 512), 512)
     here, there = ybuf.at[z_lo, :, quarter], ybuf.at[1 - z_lo, :, quarter]
@@ -387,11 +382,10 @@
 
     def pass_on(c):
         relays[c].wait_recv()
-        opp[:, parts[c]] = con_ref[1, :, parts[c]] + from_opp[:, parts[c]]
+        opp[:, parts[c]] = con_ref[2, :, parts[c]] + from_opp[:, parts[c]]
         onward[c].start()
 
     centre = jnp.sum(ybuf[z_lo], axis=1, keepdims=True) * (1.0 / HALF)
-    loads[2].wait()
     for c in range(4):
         pass_on(c)
     target(z_lo, centre)
@@ -405,7 +399,6 @@
         for r in range(TILE // 128):
             wide[pl.ds(TILE // 128 * j + r, 1), :] = value[:, r * 128 : (r + 1) * 128]
 
-    loads[3].wait()
     own.wait_recv()
 
     half = pl.ds(pl.multiple_of(x_hi * HALF, HALF), HALF)
@@ -625,6 +618,17 @@
     self_out[16:32, :] = fin[1, 1]
 
 
+def store_kernel(a, b, c, a_out, b_out, c_out, sem):
+    copies = [
+        pltpu.make_async_copy(x, y, sem.at[i])
+        for i, (x, y) in enumerate([(a, a_out), (b, b_out), (c, c_out)])
+    ]
+    for copy in copies:
+        copy.start()
+    for copy in copies:
+        copy.wait()
+
+
 def on_device(
     src_features, src_mass, section_ids, shard_counts, section_offsets, tgt_features, tgt_mass
 ):
@@ -633,13 +637,12 @@
     V, D = pltpu.VMEM, pltpu.SemaphoreType.DMA
     contributions = pl.pallas_call(
         relay_kernel,
-        out_shape=jax.ShapeDtypeStruct((4, ROWS, GROUP), F32),
+        out_shape=V((4, ROWS, GROUP), F32),
         in_specs=[pl.BlockSpec(memory_space=pltpu.SMEM)] + [hbm] * 4,
-        out_specs=hbm,
+        out_specs=vmem,
         scratch_shapes=[
             V((ROWS, WIDTH), F32), V((COMPONENTS, CAP), F32), V((1, CAP), F32),
-            V((1, CAP), jnp.int32), V((SECTIONS, COMPONENTS), F32), V((4, ROWS, GROUP), F32),
-            D((4,)), D((3,)), D((4,)),
+            V((1, CAP), jnp.int32), V((SECTIONS, COMPONENTS), F32), D((4,)), D((3,)),
         ],
         compiler_params=pltpu.CompilerParams(vmem_limit_bytes=58 * 1024 * 1024),
     )(
@@ -655,10 +658,10 @@
         out_shape=(
             V((32, 128), F32), V((8, 128), F32), V((32, 128), F32),
         ),
-        in_specs=[hbm] * 3,
+        in_specs=[vmem, hbm, hbm],
         out_specs=(vmem, vmem, vmem),
         scratch_shapes=[
-            V((2, ROWS, GROUP), F32), V((COMPONENTS, HALF), F32), V((1, HALF), F32),
+            V((COMPONENTS, HALF), F32), V((1, HALF), F32),
             V((ROWS, GROUP), F32), V((ROWS, GROUP), F32), V((ROWS, GROUP), F32),
             V((ROWS, GROUP), F32), V((2, ROWS, HALF), F32), V((ROWS, GROUP), F32),
             V((ROWS, HALF), F32),
@@ -675,12 +678,19 @@
             D((4,)), D((4,)), D((4,)), D((4,)), D((2,)), D((4,)), D((2,)), D,
             D((ITERS, 2)), D((ITERS, 2)), D((ITERS,)), D((ITERS,)), D((ITERS, 2)), D((ITERS, 2)),
             D((ITERS,)), D((ITERS,)), D((2,)), D((2,)),
-            D((4,)),
+            D((2,)),
         ],
         compiler_params=pltpu.CompilerParams(
-            collective_id=0, has_side_effects=True, vmem_limit_bytes=58 * 1024 * 1024
+            collective_id=0, has_side_effects=True, vmem_limit_bytes=50 * 1024 * 1024
         ),
     )(contributions, tgt_features, tgt_mass.reshape(1, HALF))
+    outs = pl.pallas_call(
+        store_kernel,
+        out_shape=tuple(jax.ShapeDtypeStruct(o.shape, F32) for o in outs),
+        in_specs=[vmem] * 3,
+        out_specs=(hbm, hbm, hbm),
+        scratch_shapes=[D((3,))],
+    )(*outs)
     return (outs[0].reshape(2 * GROUP), outs[1].reshape(HALF), outs[2].reshape(2 * GROUP))
 
 

time: 74.7 us -> 74.4 us (level)
    pallas_call x1, Pallas kernels: 67.7 us -> 66.6 us  [on_device(): pl.pallas_call(sinkhorn_kernel, out_shape=(V((32, 128), F32), V((8, 128),...]
    pallas_call x1 -> x2, Pallas kernels: 4.37 us -> 4.97 us  [the longest x1 3.59 us: on_device(): pl.pallas_call(relay_kernel, out_shape=V((4, ROWS, GROUP), F32), in_specs...]
    unnamed x3 -> x10, local copies, waits for them, and re-layouts: 1.81 us -> 1.79 us
where the time goes in v10:
time: 74.4 us; the launch traced here: 74.2 us
  Pallas kernels  71.5 us (96%)
  local copies, waits for them, and re-layouts  1.79 us (2%)
  between operations  0.85 us (1%)
    pallas_call x1, Pallas kernels, on_device(): pl.pallas_call(sinkhorn_kernel, out_shape=(V((32, 128), F32), V((8, 128),...  66.6 us
    pallas_call x1, Pallas kernels, on_device(): pl.pallas_call(relay_kernel, out_shape=V((4, ROWS, GROUP), F32), in_specs...  3.59 us
    unnamed x10, local copies, waits for them, and re-layouts  1.79 us

profile of v10, /device:TPU:1, one launch (start us, length us, event | category | flops | bytes accessed | tf_op | source)
XLA Modules:
  0.0 74.2 jit_solution(533018288142702743)
XLA Ops:
  0.6 0.0 copy-start
  0.6 0.0 copy-start.3
  0.7 3.6 %shard_map.94.con_ref = f32[4,56,2048]{2,1,0:T(8,128)S(1)} custom-call(s32[4]{0:T(128)} %counts_ref.1, f32[50,8192]{1,0:T(8,128)} %feats_any.1, f32[1,8192]{1,0:T(1,128)} %bitcast.8, s32[1,8192]{1,0:T(1,128)} %bitcast.9, f32[32,50]{1,0:T(8,128)} %bitcast.10), custom_call_target="tpu_custom_call" | custom-call | tf_op jit(solution)/shard_map/pallas_call | solution.py:638
  4.3 0.0 copy-done
  4.3 0.0 copy-done.3
  4.3 66.6 %shard_map.95 = (f32[32,128]{1,0:T(8,128)S(1)}, f32[8,128]{1,0:T(8,128)S(1)}, f32[32,128]{1,0:T(8,128)S(1)}) custom-call(f32[4,56,2048]{2,1,0:T(8,128)S(1)} %shard_map.94.con_ref, f32[50,1024]{1,0:T(8,128)S(1)} %copy-done, f32[1,1024]{1,0:T(1,128)S(1)} %bitcast.7), custom_call_target="tpu_custom_call" | custom-call | tf_op jit(solution)/shard_map/pallas_call | solution.py:656
  70.9 0.0 copy-start.1
  70.9 0.6 copy-done.1
  71.5 0.0 copy-start.2
  71.5 0.6 copy-done.2
  72.1 0.0 copy-start.4
  72.1 0.6 copy-done.4
  72.6 1.4 %shard_map.96 = (f32[32,128]{1,0:T(8,128)}, f32[8,128]{1,0:T(8,128)}, f32[32,128]{1,0:T(8,128)}) custom-call(f32[32,128]{1,0:T(8,128)} %copy-done.1, f32[8,128]{1,0:T(8,128)} %copy-done.4, f32[32,128]{1,0:T(8,128)} %copy-done.2), custom_call_target="tpu_custom_call" | custom-call | tf_op jit(solution)/shard_map/pallas_call | solution.py:687
Async XLA Ops:
  0.6 3.6 %copy-start = (f32[50,1024]{1,0:T(8,128)S(1)}, f32[50,1024]{1,0:T(8,128)}, u32[]{:S(2)}) copy-start(f32[50,1024]{1,0:T(8,128)} %tgt_any.1) | copy-start | bytes 614404
  0.6 3.6 %copy-start.3 = (f32[1024]{0:T(1024)S(1)}, f32[1024]{0:T(1024)}, u32[]{:S(2)}) copy-start(f32[1024]{0:T(1024)} %param.13) | copy-start | bytes 12292
  70.9 0.6 copy-start.1
  71.5 0.6 copy-start.2
  72.1 0.6 copy-start.4

commit v11 on v10

--- a/solution.py
+++ b/solution.py
@@ -120,7 +120,8 @@
     correct(feats_ref, mass_ref, ids_ref, offsets_ref, held, ready)
     for index in range(4):
         to_x, to_core = lax.rem(x_lo + index // 2, 2), lax.rem(core + index % 2, 2)
-        base = (to_x * 2 + to_core) * (2 * GROUP) + z_lo * GROUP - begin
+        straight = lax.rem(x_lo + to_core, 2) * (index // 2)
+        base = (to_x * 2 + to_core) * (2 * GROUP) + lax.rem(x_hi + straight, 2) * GROUP - begin
         contribute(held, base, count, out_ref.at[index])
 
 
@@ -299,30 +300,30 @@
 ):
     x_lo, core, z_hi, z_lo, y, x_hi = place()
     sibling = device(x_lo, 1 - core, z_hi, z_lo, y, x_hi)
-    twin = device(x_lo, core, z_hi, 1 - z_lo, y, x_hi)
+    twin = device(x_lo, core, z_hi, z_lo, y, 1 - x_hi)
     across = device(1 - x_lo, core, z_hi, z_lo, y, 1 - x_hi)
     straight = lax.rem(x_lo + core, 2)
     opposite = device(1 - x_lo, core, z_hi, z_lo, y, lax.rem(x_hi + straight, 2))
     y_hi, y_lo = lax.div(y, 2), lax.rem(y, 2)
     partner = device(
-        lax.rem(x_lo + y_hi, 2), lax.rem(core + y_lo, 2), z_hi, lax.rem(z_lo + z_hi, 2), y, x_hi
+        lax.rem(x_lo + y_hi, 2), lax.rem(core + y_lo, 2), z_hi, z_lo, y, lax.rem(x_hi + z_hi, 2)
     )
     alone = (y + z_hi) == 0
-    g = x_lo * 4 + core * 2 + z_lo
-    m = z_hi * 8 + y * 2 + x_hi
+    g = x_lo * 4 + core * 2 + x_hi
+    m = z_hi * 8 + z_lo * 4 + y
 
     def m_peer(k):
-        return device(x_lo, core, lax.div(k, 8), z_lo, lax.rem(lax.div(k, 2), 4), lax.rem(k, 2))
+        return device(x_lo, core, lax.div(k, 8), lax.rem(lax.div(k, 4), 2), lax.rem(k, 4), x_hi)
 
     def g_peer(k):
-        return device(lax.div(k, 4), lax.rem(lax.div(k, 2), 2), z_hi, lax.rem(k, 2), y, x_hi)
+        return device(lax.div(k, 4), lax.rem(lax.div(k, 2), 2), z_hi, z_lo, y, lax.rem(k, 2))
 
     m_others = [lax.rem(m + d, 16) for d in range(1, 16)]
     g_others = [lax.rem(g + d, 8) for d in range(1, 8)]
 
     barrier = pltpu.get_barrier_semaphore()
     peers = [m_peer(k) for k in m_others]
-    peers += [g_peer(k) for k in g_others] + [across]
+    peers += [g_peer(k) for k in g_others]
     for peer in peers:
         pl.semaphore_signal(barrier, inc=1, device_id=peer, device_id_type=MESH)
 
@@ -336,9 +337,9 @@
         copy.start()
     loads[0].wait()
     loads[1].wait()
-    ybuf[z_lo, 48:ROWS, :] = jnp.zeros((ROWS - 48, HALF), F32)
-    ybuf[z_lo, 0:COMPONENTS, :] = tgt_ref[...]
-    ybuf[z_lo, COMPONENTS : COMPONENTS + 1, :] = tgt_mass_ref[...]
+    ybuf[x_hi, 48:ROWS, :] = jnp.zeros((ROWS - 48, HALF), F32)
+    ybuf[x_hi, 0:COMPONENTS, :] = tgt_ref[...]
+    ybuf[x_hi, COMPONENTS : COMPONENTS + 1, :] = tgt_mass_ref[...]
 
     pl.semaphore_wait(barrier, len(peers))
 
@@ -356,8 +357,8 @@
     own = remote(con_ref.at[1], from_own, own_sem.at[0], own_sem.at[1], sibling)
     quarter = pl.ds(pl.multiple_of(core * 512, 512), 512)
     rest = pl.ds(pl.multiple_of((1 - core) * 512, 512), 512)
-    here, there = ybuf.at[z_lo, :, quarter], ybuf.at[1 - z_lo, :, quarter]
-    tgt = remote(here, here, tgt_sem.at[0], tgt_sem.at[1], twin)
+    here, there = ybuf.at[x_hi, :, quarter], ybuf.at[1 - x_hi, :, quarter]
+    tgt = remote(here, here, tgt_sem.at[0], tgt_sem.at[1], across)
     tgt.start()
     passed = remote(there, there, tgt_sem.at[2], tgt_sem.at[3], sibling)
 
@@ -385,15 +386,15 @@
         opp[:, parts[c]] = con_ref[2, :, parts[c]] + from_opp[:, parts[c]]
         onward[c].start()
 
-    centre = jnp.sum(ybuf[z_lo], axis=1, keepdims=True) * (1.0 / HALF)
+    centre = jnp.sum(ybuf[x_hi], axis=1, keepdims=True) * (1.0 / HALF)
     for c in range(4):
         pass_on(c)
-    target(z_lo, centre)
-    remote(there, there, tgt_sem.at[0], tgt_sem.at[1], twin).wait_recv()
+    target(x_hi, centre)
+    remote(there, there, tgt_sem.at[0], tgt_sem.at[1], across).wait_recv()
     passed.start()
-    handed = ybuf.at[1 - z_lo, :, rest]
+    handed = ybuf.at[1 - x_hi, :, rest]
     remote(handed, handed, tgt_sem.at[2], tgt_sem.at[3], sibling).wait_recv()
-    target(1 - z_lo, centre)
+    target(1 - x_hi, centre)
 
     def put_wide(j, value):
         for r in range(TILE // 128):
@@ -401,7 +402,7 @@
 
     own.wait_recv()
 
-    half = pl.ds(pl.multiple_of(x_hi * HALF, HALF), HALF)
+    half = pl.ds(pl.multiple_of(z_lo * HALF, HALF), HALF)
     shared = remote(xfull.at[:, half], sbuf, self_sem.at[0], self_sem.at[1], partner)
     kept_here = pltpu.make_async_copy(xfull.at[:, half], sbuf, local_sem)
 
@@ -414,11 +415,11 @@
         cells = con_ref[0, :, s] + from_own[:, s] + landed[:, s]
         xfull[:, s] = cells
         if c % 2:
-            @pl.when((x_hi == c // 2) & alone)
+            @pl.when((z_lo == c // 2) & alone)
             def _():
                 kept_here.start()
 
-            @pl.when((x_hi == c // 2) & jnp.logical_not(alone))
+            @pl.when((z_lo == c // 2) & jnp.logical_not(alone))
             def _():
                 shared.start()
 
@@ -474,7 +475,7 @@
     pot_p[...] = jnp.zeros_like(pot_p)
     pot_s[...] = jnp.zeros_like(pot_s)
 
-    half_rows = pl.ds(pl.multiple_of(x_hi * 8, 8), 8)
+    half_rows = pl.ds(pl.multiple_of(z_lo * 8, 8), 8)
 
     def finish_p(it):
         at, send, recv = p_box(it)
@@ -571,9 +572,9 @@
 
         @pl.when(it == ITERS - 1)
         def _():
-            fin[0, z_lo] = pots_f[...] * (1.0 / SCALE)
+            fin[0, x_hi] = pots_f[...] * (1.0 / SCALE)
             remote(
-                fin.at[0, z_lo], fin.at[0, z_lo], fin_send.at[0], fin_recv.at[0], twin
+                fin.at[0, x_hi], fin.at[0, x_hi], fin_send.at[0], fin_recv.at[0], twin
             ).start()
 
         @pl.when(it == 0)
@@ -587,9 +588,9 @@
 
         @pl.when(it == ITERS - 1)
         def _():
-            fin[1, z_lo] = pot_p[...] * (1.0 / SCALE)
+            fin[1, x_hi] = pot_p[...] * (1.0 / SCALE)
             remote(
-                fin.at[1, z_lo], fin.at[1, z_lo], fin_send.at[1], fin_recv.at[1], twin
+                fin.at[1, x_hi], fin.at[1, x_hi], fin_send.at[1], fin_recv.at[1], twin
             ).start()
 
         for copy in sent:
@@ -603,30 +604,19 @@
         moved = all_of(at, *to_g, send, recv)
         moved.wait_recv()
         moved.wait_send()
-    tgt_out[...] = (-TAU / SCALE) * log_sum(gb[ITERS - 1, z_lo])
+    tgt_out[...] = (-TAU / SCALE) * log_sum(gb[ITERS - 1, x_hi])
     for kind in range(2):
         remote(
-            fin.at[kind, 1 - z_lo], fin.at[kind, 1 - z_lo], fin_send.at[kind], fin_recv.at[kind],
+            fin.at[kind, 1 - x_hi], fin.at[kind, 1 - x_hi], fin_send.at[kind], fin_recv.at[kind],
             twin,
         ).wait_recv()
         remote(
-            fin.at[kind, z_lo], fin.at[kind, z_lo], fin_send.at[kind], fin_recv.at[kind], twin
+            fin.at[kind, x_hi], fin.at[kind, x_hi], fin_send.at[kind], fin_recv.at[kind], twin
         ).wait_send()
     src_out[0:16, :] = fin[0, 0]
     src_out[16:32, :] = fin[0, 1]
     self_out[0:16, :] = fin[1, 0]
     self_out[16:32, :] = fin[1, 1]
-
-
-def store_kernel(a, b, c, a_out, b_out, c_out, sem):
-    copies = [
-        pltpu.make_async_copy(x, y, sem.at[i])
-        for i, (x, y) in enumerate([(a, a_out), (b, b_out), (c, c_out)])
-    ]
-    for copy in copies:
-        copy.start()
-    for copy in copies:
-        copy.wait()
 
 
 def on_device(
@@ -684,13 +674,6 @@
             collective_id=0, has_side_effects=True, vmem_limit_bytes=50 * 1024 * 1024
         ),
     )(contributions, tgt_features, tgt_mass.reshape(1, HALF))
-    outs = pl.pallas_call(
-        store_kernel,
-        out_shape=tuple(jax.ShapeDtypeStruct(o.shape, F32) for o in outs),
-        in_specs=[vmem] * 3,
-        out_specs=(hbm, hbm, hbm),
-        scratch_shapes=[D((3,))],
-    )(*outs)
     return (outs[0].reshape(2 * GROUP), outs[1].reshape(HALF), outs[2].reshape(2 * GROUP))
 
 

time: 74.4 us -> 71.7 us (0.964)
  Pallas kernels: 71.5 us -> 69.1 us
    pallas_call x1 -> x0, Pallas kernels: 1.38 us -> none  [on_device(): pl.pallas_call(store_kernel, out_shape=tuple((jax.ShapeDtypeStruct(o.shap...]
    pallas_call x1, Pallas kernels: 66.6 us -> 65.5 us  [on_device(): pl.pallas_call(sinkhorn_kernel, out_shape=(V((32, 128), F32), V((8, 128),...]
    unnamed x10 -> x7, local copies, waits for them, and re-layouts: 1.79 us -> 1.82 us
where the time goes in v11:
time: 71.7 us; the launch traced here: 71.6 us
  Pallas kernels  69.1 us (96%)
  local copies, waits for them, and re-layouts  1.82 us (3%)
    pallas_call x1, Pallas kernels, on_device(): pl.pallas_call(sinkhorn_kernel, out_shape=(V((32, 128), F32), V((8, 128),...  65.5 us
    pallas_call x1, Pallas kernels, on_device(): pl.pallas_call(relay_kernel, out_shape=V((4, ROWS, GROUP), F32), in_specs...  3.59 us
    unnamed x7, local copies, waits for them, and re-layouts  1.82 us

profile of v11, /device:TPU:1, one launch (start us, length us, event | category | flops | bytes accessed | tf_op | source)
XLA Modules:
  0.0 71.6 jit_solution(10128819547446445303)
XLA Ops:
  0.6 0.0 copy-start
  0.6 0.0 copy-start.1
  0.7 3.6 %shard_map.94.con_ref = f32[4,56,2048]{2,1,0:T(8,128)S(1)} custom-call(s32[4]{0:T(128)} %counts_ref.1, f32[50,8192]{1,0:T(8,128)} %feats_any.1, f32[1,8192]{1,0:T(1,128)} %bitcast.11, s32[1,8192]{1,0:T(1,128)} %bitcast.12, f32[32,50]{1,0:T(8,128)} %bitcast.13), custom_call_target="tpu_custom_call" | custom-call | tf_op jit(solution)/shard_map/pallas_call | solution.py:628
  4.3 0.0 copy-done
  4.3 0.0 copy-done.1
  4.3 65.5 %shard_map.95 = (f32[32,128]{1,0:T(8,128)S(1)}, f32[8,128]{1,0:T(8,128)S(1)}, f32[32,128]{1,0:T(8,128)S(1)}) custom-call(f32[4,56,2048]{2,1,0:T(8,128)S(1)} %shard_map.94.con_ref, f32[50,1024]{1,0:T(8,128)S(1)} %copy-done, f32[1,1024]{1,0:T(1,128)S(1)} %bitcast.10), custom_call_target="tpu_custom_call" | custom-call | tf_op jit(solution)/shard_map/pallas_call | solution.py:646
  69.8 0.6 copy.13
  70.4 0.6 copy.14
  71.0 0.6 copy.15
Async XLA Ops:
  0.6 3.6 %copy-start = (f32[50,1024]{1,0:T(8,128)S(1)}, f32[50,1024]{1,0:T(8,128)}, u32[]{:S(2)}) copy-start(f32[50,1024]{1,0:T(8,128)} %tgt_any.1) | copy-start | bytes 614404
  0.6 3.6 %copy-start.1 = (f32[1024]{0:T(1024)S(1)}, f32[1024]{0:T(1024)}, u32[]{:S(2)}) copy-start(f32[1024]{0:T(1024)} %param.13) | copy-start | bytes 12292

commit v12 on v11

--- a/solution.py
+++ b/solution.py
@@ -502,6 +502,11 @@
                 if n == 0:
                     row_pass(cache_f, wide_g, (0, HALF), (0, 8), state, True, False, None)
                 moved.wait_send()
+
+            @pl.when(it == 1)
+            def _():
+                finish_p(0)
+
             for n in range(2):
                 tiles = (4 * n, 4 * n + 4)
                 row_pass(cache_f, wide_g, (HALF, GROUP), tiles, state, False, True, put_wide)
@@ -526,10 +531,6 @@
             to_rows(log_s, jnp.log2(got[COMPONENTS : COMPONENTS + 1, :]))
             upper, lower, unused = pieces(columns)
             set_left(lhs_s, 0, upper, upper, lower, log_s[...] - sq_s[...])
-
-        @pl.when(it == 1)
-        def _():
-            finish_p(0)
 
         @pl.when(it > 0)
         def _():

time: 71.7 us -> 73 us (1.018)
  Pallas kernels: 69.1 us -> 70.4 us
    pallas_call x1, Pallas kernels: 65.5 us -> 66.8 us  [on_device(): pl.pallas_call(sinkhorn_kernel, out_shape=(V((32, 128), F32), V((8, 128),...]
where the time goes in v12:
time: 73 us; the launch traced here: 72.9 us
  Pallas kernels  70.4 us (96%)
  local copies, waits for them, and re-layouts  1.82 us (2%)
    pallas_call x1, Pallas kernels, on_device(): pl.pallas_call(sinkhorn_kernel, out_shape=(V((32, 128), F32), V((8, 128),...  66.8 us
    pallas_call x1, Pallas kernels, on_device(): pl.pallas_call(relay_kernel, out_shape=V((4, ROWS, GROUP), F32), in_specs...  3.59 us
    unnamed x7, local copies, waits for them, and re-layouts  1.82 us

profile of v12, /device:TPU:1, one launch (start us, length us, event | category | flops | bytes accessed | tf_op | source)
XLA Modules:
  0.0 72.9 jit_solution(13370400436865375603)
XLA Ops:
  0.6 0.0 copy-start
  0.6 0.0 copy-start.1
  0.7 3.6 %shard_map.94.con_ref = f32[4,56,2048]{2,1,0:T(8,128)S(1)} custom-call(s32[4]{0:T(128)} %counts_ref.1, f32[50,8192]{1,0:T(8,128)} %feats_any.1, f32[1,8192]{1,0:T(1,128)} %bitcast.11, s32[1,8192]{1,0:T(1,128)} %bitcast.12, f32[32,50]{1,0:T(8,128)} %bitcast.13), custom_call_target="tpu_custom_call" | custom-call | tf_op jit(solution)/shard_map/pallas_call | solution.py:629
  4.3 0.0 copy-done
  4.3 0.0 copy-done.1
  4.3 66.8 %shard_map.95 = (f32[32,128]{1,0:T(8,128)S(1)}, f32[8,128]{1,0:T(8,128)S(1)}, f32[32,128]{1,0:T(8,128)S(1)}) custom-call(f32[4,56,2048]{2,1,0:T(8,128)S(1)} %shard_map.94.con_ref, f32[50,1024]{1,0:T(8,128)S(1)} %copy-done, f32[1,1024]{1,0:T(1,128)S(1)} %bitcast.10), custom_call_target="tpu_custom_call" | custom-call | tf_op jit(solution)/shard_map/pallas_call | solution.py:647
  71.1 0.6 copy.13
  71.7 0.6 copy.14
  72.3 0.6 copy.15
Async XLA Ops:
  0.6 3.6 %copy-start = (f32[50,1024]{1,0:T(8,128)S(1)}, f32[50,1024]{1,0:T(8,128)}, u32[]{:S(2)}) copy-start(f32[50,1024]{1,0:T(8,128)} %tgt_any.1) | copy-start | bytes 614404
  0.6 3.6 %copy-start.1 = (f32[1024]{0:T(1024)S(1)}, f32[1024]{0:T(1024)}, u32[]{:S(2)}) copy-start(f32[1024]{0:T(1024)} %param.13) | copy-start | bytes 12292
